TPU v7x, 256 devices: a whole 4x4x8 slice. The times are simulated.
256 devices in a mesh: rep: 16 (over z, x_hi), space: 16 (over y, x_lo, core).
Axes of the slice: x: 4 (x_hi: 2, x_lo: 2; x = x_hi * 2 + x_lo), y: 4, z: 8, core: 2. Of those that a mesh axis runs over, the one named last changes fastest.
Arguments:
- positions: float32 [16, 3, 32, 4, 4, 128], P('rep', None, 'space'), may hold values from 0 to 1
- velocities: float32 [16, 3, 32, 4, 4, 128], P('rep', None, 'space'), may hold values from -12 to 12
- thermal_noise: float32 [16, 1, 3, 32, 4, 4, 128], P('rep', None, None, 'space'), may hold values from -6 to 6
- counts: int32 [32, 4, 4], P('space'), may hold values from 64 to 128, as said below
- pair_flags: int32 [13, 32, 4, 4], P(None, 'space'), may hold values 0 or 1
- exit_replica: int32 [16], replicated, may hold values from 0 to 15, each once
Outputs:
- quench_pos: float32 [16, 3, 32, 4, 4, 128], P('rep', None, 'space')
- quench_vel: float32 [16, 3, 32, 4, 4, 128], P('rep', None, 'space')
- dephase_pos: float32 [16, 3, 32, 4, 4, 128], P('rep', None, 'space')
- dephase_vel: float32 [16, 3, 32, 4, 4, 128], P('rep', None, 'space')
Inputs may be any that keep to these rules, and one draw needn't show every extreme that they name: `counts`: the cell with the lowest indices of every aligned slab of 2 planes along the first dimension holds 128 atoms. `exit_replica`: every replica appears exactly once.
All inputs are finite; a program needn't handle non-finite values. No bound on the sum of `pair_flags` on one device may be relied on, other than what follows from the above.
Results may differ from a plain program's by a relative error of at most 0.0003.
Values sent between devices are 32-bit elements; how exact they have to be, the bound alone decides.
A program may use at most 128 MiB of HBM per device.

v0:
```python
import math

import jax
import jax.numpy as jnp
from jax import lax
from jax.experimental import pallas as pl
from jax.experimental.pallas import tpu as pltpu
from jax.sharding import PartitionSpec as P

QUENCH = 2
STEP_SIZE = 0.1
ALPHA_MIX = 0.25
EPSILON = 1e-06
FRICTION = math.exp(-0.2)
KICK_SCALE = math.sqrt(1.0 - FRICTION * FRICTION)

HALF_OFFSETS = (
    [(1, p, q) for p in (-1, 0, 1) for q in (-1, 0, 1)]
    + [(0, 1, q) for q in (-1, 0, 1)]
    + [(0, 0, 1)]
)
OFFSETS = [(p, q, r) for p in (-1, 0, 1) for q in (-1, 0, 1) for r in (-1, 0, 1)]
FAR = -1.0e6
LEFT = (0, 1, 2, 0, 1, 0)
RIGHT = (0, 0, 0, 1, 1, 2)
DEPTH = 48
F32, BF16 = jnp.float32, jnp.bfloat16


def flag_lookup(o):
    if o in HALF_OFFSETS:
        return HALF_OFFSETS.index(o), True
    return HALF_OFFSETS.index((-o[0], -o[1], -o[2])), False


def pieces(v):
    p1 = v.astype(BF16).astype(F32)
    r = v - p1
    p2 = r.astype(BF16).astype(F32)
    return p1, p2, r - p2


def split_rows(v, order):
    p = pieces(v)
    return jnp.concatenate([p[i] for i in order], axis=0)


def prepare_partners(pos_ref, count_ref, embed_ref, left_ref, mom_ref):
    lane = lax.broadcasted_iota(jnp.int32, (1, 128), 1)
    ones = jnp.ones((1, 128), F32)
    zeros = jnp.zeros((1, 128), F32)

    def one(j, carry):
        x = pos_ref[0, pl.ds(j, 1), :]
        y = pos_ref[1, pl.ds(j, 1), :]
        z = pos_ref[2, pl.ds(j, 1), :]
        live = lane < count_ref[j]
        norm = jnp.where(live, -(x * x + y * y + z * z), FAR)
        x = jnp.where(live, x, 0.0)
        y = jnp.where(live, y, 0.0)
        z = jnp.where(live, z, 0.0)
        e = zeros if embed_ref is None else jnp.where(live, embed_ref[pl.ds(j, 1), :], 0.0)
        v = jnp.concatenate([x, y, z, norm, ones, e, zeros, zeros], axis=0)
        p = pieces(v)
        table = jnp.concatenate([p[i] for i in LEFT], axis=0)
        left_ref[j] = table.T.astype(BF16)
        if mom_ref is not None:
            mom_ref[j] = jnp.concatenate([p[0], p[1]], axis=0).astype(BF16)
        return carry

    lax.fori_loop(0, 64, one, 0)


def centre_rows(pos_ref, i):
    x = pos_ref[0, pl.ds(i, 1), :]
    y = pos_ref[1, pl.ds(i, 1), :]
    z = pos_ref[2, pl.ds(i, 1), :]
    return x, y, z


def neighbour(c, o):
    cp, cy, cz = c // 16, (c // 4) % 4, c % 4
    return (cp + 1 + o[0]) * 16 + ((cy + o[1]) % 4 if isinstance(c, int) else ((cy + o[1] + 4) & 3)) * 4 + ((cz + o[2] + 4) & 3)


def density_kernel(pos_ref, count_ref, flag_ref, embed_ref, left_ref):
    prepare_partners(pos_ref, count_ref, None, left_ref, None)
    ones = jnp.ones((1, 128), F32)
    zeros = jnp.zeros((3, 128), F32)

    def one(c, carry):
        i = c + 16
        x, y, z = centre_rows(pos_ref, i)
        total = jnp.zeros((8, 128), F32)
        for o in OFFSETS:
            j = neighbour(c, o)
            dx, dy, dz = x - o[0], y - o[1], z - o[2]
            own = 1.0 - (dx * dx + dy * dy + dz * dz)
            if o != (0, 0, 0):
                h, forward = flag_lookup(o)
                flag = flag_ref[h, i] if forward else flag_ref[h, j]
                own = jnp.where(flag > 0, own, FAR)
            w = jnp.concatenate([2.0 * dx, 2.0 * dy, 2.0 * dz, ones, own, zeros], axis=0)
            right = split_rows(w, RIGHT).astype(BF16)
            m = jnp.dot(left_ref[j], right, preferred_element_type=F32)
            t = jnp.maximum(m, 0.0)
            if o == (0, 0, 0):
                rows = lax.broadcasted_iota(jnp.int32, (128, 128), 0)
                cols = lax.broadcasted_iota(jnp.int32, (128, 128), 1)
                t = jnp.where(rows == cols, 0.0, t)
            total = total + jnp.sum((t * t * t).reshape(16, 8, 128), axis=0)
        density = jnp.sum(total, axis=0, keepdims=True) / 128.0
        embed_ref[pl.ds(c, 1), :] = -0.25 * lax.rsqrt(1.0 + density)
        return carry

    lax.fori_loop(0, 32, one, 0)


def force_kernel(pos_ref, count_ref, flag_ref, embed_ref, force_ref, left_ref, mom_ref):
    prepare_partners(pos_ref, count_ref, embed_ref, left_ref, mom_ref)
    ones = jnp.ones((1, 128), F32)
    zero = jnp.zeros((1, 128), F32)
    lane = lax.broadcasted_iota(jnp.int32, (1, 128), 1)

    def one(c, carry):
        i = c + 16
        x, y, z = centre_rows(pos_ref, i)
        e = embed_ref[pl.ds(i, 1), :]
        fx = zero
        fy = zero
        fz = zero
        for o in OFFSETS:
            j = neighbour(c, o)
            dx, dy, dz = x - o[0], y - o[1], z - o[2]
            own = 1.0 - (dx * dx + dy * dy + dz * dz)
            if o != (0, 0, 0):
                h, forward = flag_lookup(o)
                flag = flag_ref[h, i] if forward else flag_ref[h, j]
                own = jnp.where(flag > 0, own, FAR)
            w = jnp.concatenate([2.0 * dx, 2.0 * dy, 2.0 * dz, ones, own, zero, zero, zero], axis=0)
            u = jnp.concatenate([2.0 * dx, 2.0 * dy, 2.0 * dz, ones, own + e, ones, zero, zero], axis=0)
            right = jnp.concatenate([split_rows(w, RIGHT), split_rows(u, RIGHT)], axis=1).astype(BF16)
            both = jnp.dot(left_ref[j], right, preferred_element_type=F32)
            t = jnp.maximum(both[:, :128], 0.0)
            if o == (0, 0, 0):
                rows = lax.broadcasted_iota(jnp.int32, (128, 128), 0)
                cols = lax.broadcasted_iota(jnp.int32, (128, 128), 1)
                t = jnp.where(rows == cols, 0.0, t)
            g = t * t * both[:, 128:]
            hi = g.astype(BF16)
            lo = (g - hi.astype(F32)).astype(BF16)
            mom = mom_ref[j]
            s = jnp.dot(mom, hi, preferred_element_type=F32) + jnp.dot(mom, lo, preferred_element_type=F32)
            s = s[:8] + s[8:]
            fx = fx + (dx * s[4:5] - s[0:1])
            fy = fy + (dy * s[4:5] - s[1:2])
            fz = fz + (dz * s[4:5] - s[2:3])
        scale = jnp.where(lane < count_ref[i], 24.0 / 128.0, 0.0)
        force_ref[0, pl.ds(c, 1), :] = fx * scale
        force_ref[1, pl.ds(c, 1), :] = fy * scale
        force_ref[2, pl.ds(c, 1), :] = fz * scale
        return carry

    lax.fori_loop(0, 32, one, 0)


VM = pl.BlockSpec(memory_space=pltpu.VMEM)
SM = pl.BlockSpec(memory_space=pltpu.SMEM)


def density(pos, counts, flags):
    return pl.pallas_call(
        density_kernel,
        out_shape=jax.ShapeDtypeStruct((32, 128), F32),
        in_specs=[VM, SM, SM],
        out_specs=VM,
        scratch_shapes=[pltpu.VMEM((64, 128, DEPTH), BF16)],
    )(pos, counts, flags)


def force(pos, counts, flags, embed):
    return pl.pallas_call(
        force_kernel,
        out_shape=jax.ShapeDtypeStruct((3, 32, 128), F32),
        in_specs=[VM, SM, SM, VM],
        out_specs=VM,
        scratch_shapes=[pltpu.VMEM((64, 128, DEPTH), BF16), pltpu.VMEM((64, 16, 128), BF16)],
    )(pos, counts, flags, embed)


def ring(size):
    forward = [(i, (i + 1) % size) for i in range(size)]
    backward = [(i, (i - 1) % size) for i in range(size)]
    return forward, backward


def widen(block, dim, forward, backward):
    half = block.shape[dim] // 2
    low = lax.ppermute(lax.slice_in_dim(block, half, None, axis=dim), "space", forward)
    high = lax.ppermute(lax.slice_in_dim(block, 0, half, axis=dim), "space", backward)
    return jnp.concatenate([low, block, high], axis=dim)


def body(positions, velocities, thermal_noise, counts, pair_flags, exit_replica):
    forward, backward = ring(lax.axis_size("space"))
    start_pos = positions.reshape(3, 32, 128)
    noise = thermal_noise.reshape(3, 32, 128)
    own_counts = counts.reshape(32)
    tables = widen(jnp.concatenate([own_counts[None], pair_flags.reshape(13, 32)], axis=0), 1, forward, backward)
    wide_counts, wide_flags = tables[0], tables[1:]
    occupied = (jnp.arange(128, dtype=jnp.int32) < own_counts[:, None]).astype(F32)[None]
    motion = velocities.reshape(3, 32, 128) * occupied
    wide_pos = widen(start_pos, 1, forward, backward)
    coords = start_pos
    for step in range(QUENCH):
        embed = density(wide_pos, wide_counts, wide_flags)
        wide_embed = widen(embed, 0, forward, backward)
        forces = force(wide_pos, wide_counts, wide_flags, wide_embed)
        motion = motion + STEP_SIZE * forces
        if step == 0:
            mine = lax.axis_index("rep") == exit_replica[0]
            shared = jnp.stack([start_pos, motion])
            shared = lax.psum(jnp.where(mine, shared, jnp.zeros_like(shared)), "rep")
        sums = lax.psum(jnp.stack([jnp.sum(motion * motion), jnp.sum(forces * forces)]), "space")
        mixing = jnp.sqrt(sums[0] / (sums[1] + EPSILON))
        if step == 0:
            wide = widen(jnp.concatenate([motion, forces], axis=0), 1, forward, backward)
            wide_motion = (1.0 - ALPHA_MIX) * wide[:3] + ALPHA_MIX * mixing * wide[3:]
            wide_pos = wide_pos + STEP_SIZE * wide_motion
        motion = (1.0 - ALPHA_MIX) * motion + ALPHA_MIX * mixing * forces
        coords = coords + STEP_SIZE * motion
    exit_pos, exit_motion = shared[0], shared[1]
    exit_motion = FRICTION * exit_motion + KICK_SCALE * occupied * noise
    exit_pos = exit_pos + STEP_SIZE * exit_motion
    return tuple(a.reshape(positions.shape) for a in (coords, motion, exit_pos, exit_motion))


def solution(mesh):
    atoms = P("rep", None, "space", None, None, None)
    placed = (
        atoms,
        atoms,
        P("rep", None, None, "space", None, None, None),
        P("space", None, None),
        P(None, "space", None, None),
        P(),
    )
    return jax.shard_map(body, mesh=mesh, in_specs=placed, out_specs=(atoms,) * 4, check_vma=False)
```

profile of v0, /device:TPU:8, one launch (start us, length us, event | category | flops | bytes accessed | tf_op | source)
XLA Modules:
  0.0 379.6 jit_solution(85294832497912423)
XLA Ops:
  7.2 0.0 all-reduce.2.cloned.1.call-start
  7.2 0.0 copy-start.8
  7.2 0.8 fusion.8
  8.0 0.8 collective-permute-start.1
  8.8 0.0 collective-permute-start
  8.8 0.0 copy-done.8
  8.8 0.1 copy.11
  8.9 0.6 copy-done.7
  9.5 0.1 broadcast_in_dim_reshape.4
  9.6 0.1 slice_add_fusion
  9.7 2.7 collective-permute-start.3
  12.3 0.0 collective-permute-start.2
  12.3 0.1 fusion.6
  12.4 0.1 lt.29
  12.5 1.2 collective-permute-done.3
  13.7 2.6 collective-permute-done.2
  16.3 0.7 pad_add_fusion.flag_ref
  17.0 0.6 add_bitcast_fusion.count_ref
  17.6 0.0 collective-permute-done.1
  17.6 0.0 collective-permute-done
  17.6 0.0 copy-done.1
  17.6 0.6 pad_maximum_fusion.1.pos_ref
  18.2 22.5 %shard_map.93 = f32[32,128]{1,0:T(8,128)} custom-call(f32[3,64,128]{2,1,0:T(8,128)} %pad_maximum_fusion.1.pos_ref, s32[64]{0:T(128)} %add_bitcast_fusion.count_ref, s32[13,64]{1,0:T(8,128)} %pad_add_fusion.flag_ref), custom_call_target="tpu_custom_call" | custom-call | tf_op jit(solution)/shard_map/pallas_call | solution.py:172
  40.7 0.7 fusion.10
  41.4 0.0 collective-permute-start.5
  41.5 0.5 collective-permute-start.4
  42.0 0.1 fusion.5
  42.0 0.7 copy-done.9
  42.7 0.1 collective-permute-done.5
  42.8 2.7 collective-permute-done.4
  45.5 0.0 copy-done.3
  45.5 0.6 pad_maximum_fusion.3.embed_ref
  46.1 47.4 %shard_map.94 = f32[3,32,128]{2,1,0:T(8,128)} custom-call(f32[3,64,128]{2,1,0:T(8,128)} %pad_maximum_fusion.1.pos_ref, s32[64]{0:T(128)} %add_bitcast_fusion.count_ref, s32[13,64]{1,0:T(8,128)} %pad_add_fusion.flag_ref, f32[64,128]{1,0:T(8,128)} %pad_maximum_fusion.3.embed_ref), custom_call_target="tpu_custom_call" | custom-call | tf_op jit(solution)/shard_map/pallas_call | solution.py:182
  93.5 0.0 copy-done.6
  93.5 1.5 multiply_reduce_fusion.3
  95.0 0.0 copy-done
  95.0 0.1 collective-permute-start.7
  95.1 1.4 pad_maximum_fusion.5
  96.5 0.5 collective-permute-start.6
  97.0 29.8 %psum.21 = f32[2]{0:T(128)S(1)} all-reduce(f32[2]{0:T(128)S(1)} %pad_maximum_fusion.5), channel_id=1, replica_groups=mesh['rep'=16,'space'=16] {'space'}, use_global_device_ids=true, to_apply=%region_2.3 | all-reduce | flops 2 | bytes 16 | tf_op jit(solution)/shard_map/psum | solution.py:224
  126.8 0.6 fusion.12
  128.8 0.0 collective-permute-done.7
  128.8 0.0 collective-permute-done.6
  128.8 0.7 fusion.2.pos_ref
  129.5 22.5 %shard_map.95 = f32[32,128]{1,0:T(8,128)} custom-call(f32[3,64,128]{2,1,0:T(8,128)} %fusion.2.pos_ref, s32[64]{0:T(128)} %add_bitcast_fusion.count_ref, s32[13,64]{1,0:T(8,128)} %pad_add_fusion.flag_ref), custom_call_target="tpu_custom_call" | custom-call | tf_op jit(solution)/shard_map/pallas_call | solution.py:172
  152.0 0.7 fusion.9
  152.7 0.5 collective-permute-start.9
  153.2 0.0 collective-permute-start.8
  153.2 0.6 maximum_select_fusion
  153.9 0.7 collective-permute-done.9
  154.6 4.0 %collective-permute-done.8 = f32[16,128]{1,0:T(8,128)S(1)} collective-permute-done((f32[16,128]{1,0:T(8,128)S(1)}, f32[16,128]{1,0:T(8,128)S(1)}, u32[]{:S(2)}, u32[]{:S(2)}) %collective-permute-start.8) | collective-permute-done | bytes 8224 | tf_op jit(solution)/shard_map/ppermute | solution.py:199
  158.5 0.0 copy-done.4
  158.5 0.6 pad_maximum_fusion.4.embed_ref
  159.1 47.4 %shard_map.96 = f32[3,32,128]{2,1,0:T(8,128)} custom-call(f32[3,64,128]{2,1,0:T(8,128)} %fusion.2.pos_ref, s32[64]{0:T(128)} %add_bitcast_fusion.count_ref, s32[13,64]{1,0:T(8,128)} %pad_add_fusion.flag_ref, f32[64,128]{1,0:T(8,128)} %pad_maximum_fusion.4.embed_ref), custom_call_target="tpu_custom_call" | custom-call | tf_op jit(solution)/shard_map/pallas_call | solution.py:182
  206.5 1.4 multiply_reduce_fusion.1
  207.9 1.4 pad_maximum_fusion.6
  209.3 0.0 all-reduce.2.cloned.1.call-update
  209.3 26.5 %psum.22 = f32[2]{0:T(128)S(1)} all-reduce(f32[2]{0:T(128)S(1)} %pad_maximum_fusion.6), channel_id=1, replica_groups=mesh['rep'=16,'space'=16] {'space'}, use_global_device_ids=true, to_apply=%region_5.6 | all-reduce | flops 2 | bytes 16 | tf_op jit(solution)/shard_map/psum | solution.py:224
  235.9 0.6 fusion.11
  237.8 0.0 copy-done.2
  237.8 0.7 multiply_add_fusion.1
  238.5 132.8 %all-reduce.2.cloned.1.call-done = f32[2,3,32,128]{3,2,1,0:T(8,128)} async-done(((f32[2,3,32,128]{3,2,1,0:T(8,128)}), f32[2,3,32,128]{3,2,1,0:T(8,128)}) %all-reduce.2.cloned.1.call-update) | async-done | bytes 98320 | tf_op jit(solution)/shard_map/psum | solution.py:223
  371.2 0.8 slice_multiply_fusion.2
  372.1 0.7 multiply_add_fusion
  (12 shorter events, 0.0 us)
Async XLA Ops:
  7.2 364.1 %all-reduce.2.cloned.1.call-start = ((), (), s32[]{:S(2)}) async-start(), calls=%async_computation | async-start | bytes 196608 | tf_op jit(solution)/shard_map/psum | solution.py:223
  7.2 1.6 copy-start.8
  8.0 9.6 %collective-permute-start.1 = (f32[3,16,128]{2,1,0:T(8,128)S(1)}, f32[3,16,128]{2,1,0:T(8,128)S(1)}, u32[]{:S(2)}, u32[]{:S(2)}) collective-permute-start(f32[3,16,128]{2,1,0:T(8,128)S(1)} %get-tuple-element.19), channel_id=1, source_target_pairs={{0,15},{1,0},{2,1},{3,2},{4,3},{5,4},{6,5},{7,6},{8,7},{9,8},{10,9... | collective-permute-start | bytes 73736 | tf_op jit(solution)/shard_map/ppermute | solution.py:200
  8.8 8.8 %collective-permute-start = (f32[3,16,128]{2,1,0:T(8,128)S(1)}, f32[3,16,128]{2,1,0:T(8,128)S(1)}, u32[]{:S(2)}, u32[]{:S(2)}) collective-permute-start(f32[3,16,128]{2,1,0:T(8,128)S(1)} %get-tuple-element.18), channel_id=1, source_target_pairs={{0,1},{1,2},{2,3},{3,4},{4,5},{5,6},{6,7},{7,8},{8,9},{9,10},{10,1... | collective-permute-start | bytes 73736 | tf_op jit(solution)/shard_map/ppermute | solution.py:199
  8.8 0.7 copy-start.7
  9.7 7.9 %copy-start.1 = (f32[1,3,2,4,4,128]{5,4,3,2,1,0:T(4,128)S(1)}, f32[1,3,2,4,4,128]{5,4,3,2,1,0:T(4,128)}, u32[]{:S(2)}) copy-start(f32[1,3,2,4,4,128]{5,4,3,2,1,0:T(4,128)} %param.6) | copy-start | bytes 147460
  9.7 4.0 %collective-permute-start.3 = (s32[14,16]{1,0:T(8,128)S(1)}, s32[14,16]{1,0:T(8,128)S(1)}, u32[]{:S(2)}, u32[]{:S(2)}) collective-permute-start(s32[14,16]{1,0:T(8,128)S(1)} %get-tuple-element.25), channel_id=1, source_target_pairs={{0,15},{1,0},{2,1},{3,2},{4,3},{5,4},{6,5},{7,6},{8,7},{9,8},{10,9... | collective-permute-start | bytes 2696 | tf_op jit(solution)/shard_map/ppermute | solution.py:200
  12.3 4.0 %collective-permute-start.2 = (s32[14,16]{1,0:T(8,128)S(1)}, s32[14,16]{1,0:T(8,128)S(1)}, u32[]{:S(2)}, u32[]{:S(2)}) collective-permute-start(s32[14,16]{1,0:T(8,128)S(1)} %get-tuple-element.24), channel_id=1, source_target_pairs={{0,1},{1,2},{2,3},{3,4},{4,5},{5,6},{6,7},{7,8},{8,9},{9,10},{10,1... | collective-permute-start | bytes 2696 | tf_op jit(solution)/shard_map/ppermute | solution.py:199
  41.4 4.1 %copy-start.3 = (f32[32,128]{1,0:T(8,128)S(1)}, f32[32,128]{1,0:T(8,128)}, u32[]{:S(2)}) copy-start(f32[32,128]{1,0:T(8,128)} %shard_map.93) | copy-start | bytes 49156
  41.4 1.4 collective-permute-start.5
  41.5 4.0 %collective-permute-start.4 = (f32[16,128]{1,0:T(8,128)S(1)}, f32[16,128]{1,0:T(8,128)S(1)}, u32[]{:S(2)}, u32[]{:S(2)}) collective-permute-start(f32[16,128]{1,0:T(8,128)S(1)} %get-tuple-element.22), channel_id=1, source_target_pairs={{0,1},{1,2},{2,3},{3,4},{4,5},{5,6},{6,7},{7,8},{8,9},{9,10},{10,1... | collective-permute-start | bytes 24584 | tf_op jit(solution)/shard_map/ppermute | solution.py:199
  42.0 0.7 copy-start.9
  46.1 47.4 %copy-start.6 = (f32[1,3,2,4,4,128]{5,4,3,2,1,0:T(4,128)S(1)}, f32[1,3,2,4,4,128]{5,4,3,2,1,0:T(4,128)}, u32[]{:S(2)}) copy-start(f32[1,3,2,4,4,128]{5,4,3,2,1,0:T(4,128)} %param.7) | copy-start | bytes 147460
  93.5 1.5 copy-start
  95.0 33.7 %collective-permute-start.7 = (f32[6,16,128]{2,1,0:T(8,128)S(1)}, f32[6,16,128]{2,1,0:T(8,128)S(1)}, u32[]{:S(2)}, u32[]{:S(2)}) collective-permute-start(f32[6,16,128]{2,1,0:T(8,128)S(1)} %get-tuple-element.16), channel_id=1, source_target_pairs={{0,15},{1,0},{2,1},{3,2},{4,3},{5,4},{6,5},{7,6},{8,7},{9,8},{10,9... | collective-permute-start | bytes 147464 | tf_op jit(solution)/shard_map/ppermute | solution.py:200
  96.5 32.3 %collective-permute-start.6 = (f32[6,16,128]{2,1,0:T(8,128)S(1)}, f32[6,16,128]{2,1,0:T(8,128)S(1)}, u32[]{:S(2)}, u32[]{:S(2)}) collective-permute-start(f32[6,16,128]{2,1,0:T(8,128)S(1)} %get-tuple-element.15), channel_id=1, source_target_pairs={{0,1},{1,2},{2,3},{3,4},{4,5},{5,6},{6,7},{7,8},{8,9},{9,10},{10,1... | collective-permute-start | bytes 147464 | tf_op jit(solution)/shard_map/ppermute | solution.py:199
  152.7 1.9 collective-permute-start.9
  153.2 5.3 %collective-permute-start.8 = (f32[16,128]{1,0:T(8,128)S(1)}, f32[16,128]{1,0:T(8,128)S(1)}, u32[]{:S(2)}, u32[]{:S(2)}) collective-permute-start(f32[16,128]{1,0:T(8,128)S(1)} %get-tuple-element.20), channel_id=1, source_target_pairs={{0,1},{1,2},{2,3},{3,4},{4,5},{5,6},{6,7},{7,8},{8,9},{9,10},{10,1... | collective-permute-start | bytes 24584 | tf_op jit(solution)/shard_map/ppermute | solution.py:199
  153.2 5.3 %copy-start.4 = (f32[32,128]{1,0:T(8,128)S(1)}, f32[32,128]{1,0:T(8,128)}, u32[]{:S(2)}) copy-start(f32[32,128]{1,0:T(8,128)} %shard_map.95) | copy-start | bytes 49156
  209.3 28.5 %copy-start.2 = (f32[3,32,128]{2,1,0:T(8,128)S(1)}, f32[3,32,128]{2,1,0:T(8,128)}, u32[]{:S(2)}) copy-start(f32[3,32,128]{2,1,0:T(8,128)} %shard_map.96) | copy-start | bytes 147460
  238.5 133.6 %copy-start.5 = (f32[1,1,3,2,4,4,128]{6,5,4,3,2,1,0:T(4,128)S(1)}, f32[1,1,3,2,4,4,128]{6,5,4,3,2,1,0:T(4,128)}, u32[]{:S(2)}) copy-start(f32[1,1,3,2,4,4,128]{6,5,4,3,2,1,0:T(4,128)} %param.8) | copy-start | bytes 147460
Sparse Core Ops, SparseCore 0:
  209.5 161.7 all-reduce.1
where the time goes:
time: 380 us
  waiting for transfers between devices  144 us (38%)
  Pallas kernels  140 us (37%)
  blocking collectives  56.3 us (15%)
  between operations  16.9 us (4%)
  other arithmetic  12.5 us (3%)
  starting transfers between devices  5.14 us (1%)
  local copies, waits for them, and re-layouts  4.91 us (1%)
    psum x1, waiting for transfers between devices, body(): shared = lax.psum(jnp.where(mine, shared, jnp.zeros_like(shared)), 'rep')  133 us
    pallas_call x2, Pallas kernels, force(): pl.pallas_call(force_kernel, out_shape=jax.ShapeDtypeStruct((3, 32, 128),...  94.8 us
    psum x2, blocking collectives, body(): lax.psum(jnp.stack([jnp.sum(motion * motion), jnp.sum(forces * forces)]),...  56.3 us
    pallas_call x2, Pallas kernels, density(): pl.pallas_call(density_kernel, out_shape=jax.ShapeDtypeStruct((32, 128),...  45 us
    ppermute x5, waiting for transfers between devices, widen(): lax.ppermute(lax.slice_in_dim(block, half, None, axis=dim), 'space', forw...  9.25 us
  transfers between devices with their start and end apart: 11, of which 7 were waited for; matrix products, arithmetic and copies ran while one was open for 1% of the time, Pallas kernels for 0%

commit v1 on v0

v1 whole, which is shorter than its diff:
```python
import functools
import math

import jax
import jax.numpy as jnp
from jax import lax
from jax.experimental import pallas as pl
from jax.experimental.pallas import tpu as pltpu
from jax.sharding import PartitionSpec as P

QUENCH = 2
STEP_SIZE = 0.1
ALPHA_MIX = 0.25
EPSILON = 1e-06
FRICTION = math.exp(-0.2)
KICK_SCALE = math.sqrt(1.0 - FRICTION * FRICTION)

HALF_OFFSETS = (
    [(1, p, q) for p in (-1, 0, 1) for q in (-1, 0, 1)]
    + [(0, 1, q) for q in (-1, 0, 1)]
    + [(0, 0, 1)]
)
OFFSETS = [(p, q, r) for p in (-1, 0, 1) for q in (-1, 0, 1) for r in (-1, 0, 1)]
FAR = -1.0e6
LEFT = (0, 1, 2, 0, 1, 0)
RIGHT = (0, 0, 0, 1, 1, 2)
DEPTH = 48
CHUNK = 128
UNROLL = 8
F32, BF16 = jnp.float32, jnp.bfloat16


def flag_lookup(o):
    if o in HALF_OFFSETS:
        return HALF_OFFSETS.index(o), True
    return HALF_OFFSETS.index((-o[0], -o[1], -o[2])), False


def pieces(v):
    p1 = v.astype(BF16).astype(F32)
    r = v - p1
    p2 = r.astype(BF16).astype(F32)
    return p1, p2, r - p2


def split_rows(v, order):
    p = pieces(v)
    return jnp.concatenate([p[i] for i in order], axis=0)


def prepare_partners(pos_ref, count_ref, embed_ref, left_ref, spread_ref):
    lane = lax.broadcasted_iota(jnp.int32, (1, 128), 1)
    ones = jnp.ones((1, 128), F32)
    zeros = jnp.zeros((1, 128), F32)

    def one(j, carry):
        x = pos_ref[0, pl.ds(j, 1), :]
        y = pos_ref[1, pl.ds(j, 1), :]
        z = pos_ref[2, pl.ds(j, 1), :]
        live = lane < count_ref[j]
        norm = jnp.where(live, -(x * x + y * y + z * z), FAR)
        x = jnp.where(live, x, 0.0)
        y = jnp.where(live, y, 0.0)
        z = jnp.where(live, z, 0.0)
        e = zeros if embed_ref is None else jnp.where(live, embed_ref[pl.ds(j, 1), :], 0.0)
        v = jnp.concatenate([x, y, z, norm, ones, e, zeros, zeros], axis=0)
        p = pieces(v)
        rows = [p[i] for i in LEFT]
        if spread_ref is not None:
            rows.append(v)
        table = jnp.concatenate(rows, axis=0).T
        left_ref[j] = table[:, :DEPTH].astype(BF16)
        if spread_ref is not None:
            for k in range(3):
                spread_ref[j, k] = jnp.broadcast_to(table[:, DEPTH + k : DEPTH + k + 1], (128, 128))
        return carry

    lax.fori_loop(0, 64, one, 0, unroll=UNROLL)


def centre(pos_ref, i, off_ref):
    rows = [pos_ref[k, pl.ds(i, 1), :] for k in range(3)]
    ones = jnp.ones((1, 128), F32)
    base = jnp.concatenate([2.0 * a for a in rows] + [ones, jnp.zeros((4, 128), F32)], axis=0)
    own = jnp.ones((32, 128), F32)
    for k in range(3):
        gap = rows[k] - off_ref[k]
        own = own - gap * gap
    return rows, base, own


def column(o, extra=0.0):
    row = lax.broadcasted_iota(jnp.int32, (8, 128), 0)
    col = jnp.zeros((8, 128), F32)
    for k in range(3):
        if o[k]:
            col = jnp.where(row == k, -2.0 * o[k], col)
    if extra:
        col = jnp.where(row == 5, extra, col)
    return col


def fill_offsets(off_ref):
    row = lax.broadcasted_iota(jnp.int32, (32, 128), 0)
    third = ((row // 9) - 1, (row // 3) % 3 - 1, row % 3 - 1)
    for k in range(3):
        off_ref[k] = third[k].astype(F32)


def place(c, d):
    cp, cy, cz = c // 16, (c // 4) & 3, c & 3
    return (cp + 1 + d[0]) * 16 + ((cy + d[1] + 4) & 3) * 4 + ((cz + d[2] + 4) & 3)


def flagged(flag_ref, i, j, o, own):
    if o == (0, 0, 0):
        return own
    h, forward = flag_lookup(o)
    flag = flag_ref[h, i] if forward else flag_ref[h, j]
    return jnp.where(flag > 0, own, FAR)


def not_self(t, first):
    rows = lax.broadcasted_iota(jnp.int32, t.shape, 0) + first
    cols = lax.broadcasted_iota(jnp.int32, t.shape, 1)
    return jnp.where(rows == cols, 0.0, t)


def fold(a):
    return jnp.sum(a.reshape(a.shape[0] // 8, 8, 128), axis=0)


def density_kernel(pos_ref, count_ref, flag_ref, embed_ref, left_ref, off_ref):
    prepare_partners(pos_ref, count_ref, None, left_ref, None)
    fill_offsets(off_ref)
    fifth = lax.broadcasted_iota(jnp.int32, (8, 128), 0) == 4

    def one(q, carry):
        c0 = 2 * q
        sets = [centre(pos_ref, c0 + 16 + k, off_ref) for k in (0, 1)]
        totals = [jnp.zeros((8, 128), F32), jnp.zeros((8, 128), F32)]
        for ox in (-1, 0, 1):
            for oy in (-1, 0, 1):
                for dz in (-1, 0, 1, 2):
                    j = place(c0, (ox, oy, dz))
                    used = [k for k in (0, 1) if -1 <= dz - k <= 1]
                    ws = []
                    for k in used:
                        o = (ox, oy, dz - k)
                        n = OFFSETS.index(o)
                        own = flagged(flag_ref, c0 + 16 + k, j, o, sets[k][2][n : n + 1])
                        ws.append(jnp.where(fifth, own, sets[k][1] + column(o)))
                    right = jnp.concatenate([split_rows(w, RIGHT) for w in ws], axis=1).astype(BF16)
                    for first in range(0, 128, CHUNK):
                        m = jnp.dot(left_ref[j, first : first + CHUNK], right, preferred_element_type=F32)
                        for n, k in enumerate(used):
                            t = jnp.maximum(m[:, 128 * n : 128 * n + 128], 0.0)
                            if (ox, oy, dz) == (0, 0, k):
                                t = not_self(t, first)
                            totals[k] = totals[k] + fold(t * t * t)
        for k in (0, 1):
            density = jnp.sum(totals[k], axis=0, keepdims=True) / 128.0
            embed_ref[pl.ds(c0 + k, 1), :] = -0.25 * lax.rsqrt(1.0 + density)
        return carry

    lax.fori_loop(0, 16, one, 0)


def force_kernel(pos_ref, count_ref, flag_ref, embed_ref, force_ref, left_ref, spread_ref, off_ref):
    prepare_partners(pos_ref, count_ref, embed_ref, left_ref, spread_ref)
    fill_offsets(off_ref)
    lane = lax.broadcasted_iota(jnp.int32, (1, 128), 1)
    fifth = lax.broadcasted_iota(jnp.int32, (8, 128), 0) == 4

    def one(c, carry):
        i = c + 16
        rows, base, owns = centre(pos_ref, i, off_ref)
        e = embed_ref[pl.ds(i, 1), :]
        total = [jnp.zeros((8, 128), F32) for _ in range(3)]
        for n, o in enumerate(OFFSETS):
            j = place(c, o)
            own = flagged(flag_ref, i, j, o, owns[n : n + 1])
            w = jnp.where(fifth, own, base + column(o))
            u = jnp.where(fifth, own + e, base + column(o, 1.0))
            right = jnp.concatenate([split_rows(w, RIGHT), split_rows(u, RIGHT)], axis=1).astype(BF16)
            amount = jnp.zeros((8, 128), F32)
            for first in range(0, 128, CHUNK):
                both = jnp.dot(left_ref[j, first : first + CHUNK], right, preferred_element_type=F32)
                t = jnp.maximum(both[:, :128], 0.0)
                if o == (0, 0, 0):
                    t = not_self(t, first)
                g = t * t * both[:, 128:]
                amount = amount + fold(g)
                for k in range(3):
                    total[k] = total[k] - fold(g * spread_ref[j, k, first : first + CHUNK])
            for k in range(3):
                total[k] = total[k] + (rows[k] - o[k]) * amount
        scale = jnp.where(lane < count_ref[i], 24.0 / 128.0, 0.0)
        for k in range(3):
            force_ref[k, pl.ds(c, 1), :] = jnp.sum(total[k], axis=0, keepdims=True) * scale
        return carry

    lax.fori_loop(0, 32, one, 0)


VM = pl.BlockSpec(memory_space=pltpu.VMEM)
SM = pl.BlockSpec(memory_space=pltpu.SMEM)


def density(pos, counts, flags):
    return pl.pallas_call(
        density_kernel,
        out_shape=jax.ShapeDtypeStruct((32, 128), F32),
        in_specs=[VM, SM, SM],
        out_specs=VM,
        scratch_shapes=[pltpu.VMEM((64, 128, DEPTH), BF16), pltpu.VMEM((3, 32, 128), F32)],
        compiler_params=pltpu.CompilerParams(vmem_limit_bytes=40 << 20),
        cost_estimate=pl.CostEstimate(flops=20_000_000_000, bytes_accessed=200_000, transcendentals=0),
    )(pos, counts, flags)


def force(pos, counts, flags, embed):
    return pl.pallas_call(
        force_kernel,
        out_shape=jax.ShapeDtypeStruct((3, 32, 128), F32),
        in_specs=[VM, SM, SM, VM],
        out_specs=VM,
        scratch_shapes=[
            pltpu.VMEM((64, 128, DEPTH), BF16),
            pltpu.VMEM((64, 3, 128, 128), F32),
            pltpu.VMEM((3, 32, 128), F32),
        ],
        compiler_params=pltpu.CompilerParams(vmem_limit_bytes=40 << 20),
        cost_estimate=pl.CostEstimate(flops=40_000_000_000, bytes_accessed=200_000, transcendentals=0),
    )(pos, counts, flags, embed)


MESH = pl.DeviceIdType.MESH


def peer(place):
    return (lax.axis_index("rep"), place)


def greet(places):
    barrier = pltpu.get_barrier_semaphore()
    for place in places:
        pl.semaphore_signal(barrier, inc=1, device_id=peer(place), device_id_type=MESH)
    pl.semaphore_wait(barrier, len(places))


def remote(source, target, send_sem, recv_sem, place):
    return pltpu.make_async_remote_copy(
        src_ref=source,
        dst_ref=target,
        send_sem=send_sem,
        recv_sem=recv_sem,
        device_id=peer(place),
        device_id_type=MESH,
    )


def sides(size):
    me = lax.axis_index("space")
    return lax.rem(me + size - 1, size), lax.rem(me + 1, size)


def start_kernel(size, pos_ref, table_ref, wide_ref, tables_ref, low_pos, high_pos, send_sem, recv_sem):
    left, right = sides(size)
    greet((left, right))
    copies = (
        remote(pos_ref.at[:, pl.ds(16, 16), :], low_pos, send_sem.at[0], recv_sem.at[0], right),
        remote(pos_ref.at[:, pl.ds(0, 16), :], high_pos, send_sem.at[1], recv_sem.at[1], left),
        remote(table_ref, tables_ref.at[0], send_sem.at[2], recv_sem.at[2], right),
        remote(table_ref, tables_ref.at[2], send_sem.at[3], recv_sem.at[3], left),
    )
    for copy in copies:
        copy.start()
    wide_ref[:, 16:48, :] = pos_ref[...]
    tables_ref[1] = table_ref[...]
    for copy in copies:
        copy.wait()
    wide_ref[:, 0:16, :] = low_pos[...]
    wide_ref[:, 48:64, :] = high_pos[...]


def embed_kernel(size, embed_ref, wide_ref, low, high, send_sem, recv_sem):
    left, right = sides(size)
    greet((left, right))
    copies = (
        remote(embed_ref.at[pl.ds(16, 16), :], low, send_sem.at[0], recv_sem.at[0], right),
        remote(embed_ref.at[pl.ds(0, 16), :], high, send_sem.at[1], recv_sem.at[1], left),
    )
    for copy in copies:
        copy.start()
    wide_ref[16:48, :] = embed_ref[...]
    for copy in copies:
        copy.wait()
    wide_ref[0:16, :] = low[...]
    wide_ref[48:64, :] = high[...]


def squares(a):
    return jnp.sum(jnp.sum(a * a, axis=0), axis=0, keepdims=True)


def mix_kernel(size, last, vel_ref, force_ref, wide_ref, new_pos_ref, new_vel_ref, part, slots, low, high, send_sem, recv_sem):
    me = lax.axis_index("space")
    places = [lax.rem(me + shift, size) for shift in range(1, size)]
    left, right = places[-1], places[0]
    motion, forces = vel_ref[...], force_ref[...]
    part[...] = jnp.concatenate([squares(motion), squares(forces), jnp.zeros((6, 128), F32)], axis=0)
    greet(places)
    copies = [
        remote(part, slots.at[shift], send_sem.at[shift], recv_sem.at[shift], place)
        for shift, place in enumerate(places)
    ]
    if not last:
        for k, source in enumerate((vel_ref, force_ref)):
            copies.append(
                remote(source.at[:, pl.ds(16, 16), :], low.at[k], send_sem.at[size + 2 * k], recv_sem.at[size + 2 * k], right)
            )
            copies.append(
                remote(source.at[:, pl.ds(0, 16), :], high.at[k], send_sem.at[size + 2 * k + 1], recv_sem.at[size + 2 * k + 1], left)
            )
    for copy in copies:
        copy.start()
    for copy in copies:
        copy.wait()
    total = part[...]
    for shift in range(size - 1):
        total = total + slots[shift]
    total = jnp.sum(total, axis=1, keepdims=True)
    mixing = ALPHA_MIX * jnp.sqrt(total[0:1] / (total[1:2] + EPSILON))
    mixing = mixing[None]
    new = (1.0 - ALPHA_MIX) * motion + mixing * forces
    new_vel_ref[...] = new
    moved = wide_ref[:, 16:48, :] + STEP_SIZE * new
    if last:
        new_pos_ref[...] = moved
    else:
        new_pos_ref[:, 16:48, :] = moved
        for k, (face, rows) in enumerate(((low, slice(0, 16)), (high, slice(48, 64)))):
            vel = (1.0 - ALPHA_MIX) * face[0] + mixing * face[1]
            new_pos_ref[:, rows, :] = wide_ref[:, rows, :] + STEP_SIZE * vel


def comm_params(ident):
    return pltpu.CompilerParams(collective_id=ident, has_side_effects=True)


def shaped(*shape, dtype=F32):
    return jax.ShapeDtypeStruct(shape, dtype)


def start_halo(size, pos, table):
    return pl.pallas_call(
        functools.partial(start_kernel, size),
        out_shape=(shaped(3, 64, 128), shaped(3, *table.shape, dtype=jnp.int32)),
        in_specs=[VM, VM],
        out_specs=(VM, VM),
        scratch_shapes=[
            pltpu.VMEM((3, 16, 128), F32),
            pltpu.VMEM((3, 16, 128), F32),
            pltpu.SemaphoreType.DMA((4,)),
            pltpu.SemaphoreType.DMA((4,)),
        ],
        compiler_params=comm_params(1),
    )(pos, table)


def embed_halo(size, embed):
    return pl.pallas_call(
        functools.partial(embed_kernel, size),
        out_shape=shaped(64, 128),
        in_specs=[VM],
        out_specs=VM,
        scratch_shapes=[
            pltpu.VMEM((16, 128), F32),
            pltpu.VMEM((16, 128), F32),
            pltpu.SemaphoreType.DMA((2,)),
            pltpu.SemaphoreType.DMA((2,)),
        ],
        compiler_params=comm_params(2),
    )(embed)


def mix(size, last, motion, forces, wide_pos):
    return pl.pallas_call(
        functools.partial(mix_kernel, size, last),
        out_shape=(shaped(3, 32 if last else 64, 128), shaped(3, 32, 128)),
        in_specs=[VM, VM, VM],
        out_specs=(VM, VM),
        scratch_shapes=[
            pltpu.VMEM((8, 128), F32),
            pltpu.VMEM((size - 1, 8, 128), F32),
            pltpu.VMEM((2, 3, 16, 128), F32),
            pltpu.VMEM((2, 3, 16, 128), F32),
            pltpu.SemaphoreType.DMA((size + 4,)),
            pltpu.SemaphoreType.DMA((size + 4,)),
        ],
        compiler_params=comm_params(3 + int(last)),
    )(motion, forces, wide_pos)


def gather_four(value, stage):
    size = lax.axis_size("rep")
    arrived = [lax.ppermute(value, "rep", [(i, i ^ (stage * k)) for i in range(size)]) for k in (1, 2, 3)]
    return value + arrived[0] + arrived[1] + arrived[2]


def body(positions, velocities, thermal_noise, counts, pair_flags, exit_replica):
    size = lax.axis_size("space")
    mine = lax.axis_index("rep") == exit_replica[0]
    start_pos = positions.reshape(3, 32, 128)
    noise = thermal_noise.reshape(3, 32, 128)
    own_counts = counts.reshape(32)
    table = jnp.concatenate([own_counts[None], pair_flags.reshape(13, 32)], axis=0)
    table = jnp.pad(table, ((0, 2), (0, 96)))
    wide_pos, tables = start_halo(size, start_pos, table)
    tables = jnp.concatenate([tables[0, :14, 16:32], tables[1, :14, :32], tables[2, :14, :16]], axis=1)
    wide_counts, wide_flags = tables[0], tables[1:]
    occupied = (jnp.arange(128, dtype=jnp.int32) < own_counts[:, None]).astype(F32)[None]
    motion = velocities.reshape(3, 32, 128) * occupied
    for step in range(QUENCH):
        last = step == QUENCH - 1
        embed = density(wide_pos, wide_counts, wide_flags)
        if last:
            shared = gather_four(shared, 1)
            embed, shared = lax.optimization_barrier((embed, shared))
        wide_embed = embed_halo(size, embed)
        forces = force(wide_pos, wide_counts, wide_flags, wide_embed)
        if last:
            shared = gather_four(shared, 4)
            forces, shared = lax.optimization_barrier((forces, shared))
        motion = motion + STEP_SIZE * forces
        if not last:
            shared = jnp.concatenate([start_pos, motion], axis=0)
            shared = jnp.where(mine, shared, jnp.zeros_like(shared))
        wide_pos, motion = mix(size, last, motion, forces, wide_pos)
    exit_motion = FRICTION * shared[3:] + KICK_SCALE * occupied * noise
    exit_pos = shared[:3] + STEP_SIZE * exit_motion
    return tuple(a.reshape(positions.shape) for a in (wide_pos, motion, exit_pos, exit_motion))


def solution(mesh):
    atoms = P("rep", None, "space", None, None, None)
    placed = (
        atoms,
        atoms,
        P("rep", None, None, "space", None, None, None),
        P("space", None, None),
        P(None, "space", None, None),
        P(),
    )
    return jax.shard_map(body, mesh=mesh, in_specs=placed, out_specs=(atoms,) * 4, check_vma=False)
```

time: 380 us -> 170 us (0.45)
  waiting for transfers between devices: 144 us -> 0.02 us
  blocking collectives: 56.3 us -> 0 us
  between operations: 16.9 us -> 0.95 us
  other arithmetic: 12.5 us -> 1.06 us
  starting transfers between devices: 5.14 us -> 12.3 us
  local copies, waits for them, and re-layouts: 4.91 us -> 11.4 us
    psum x1 -> x0, waiting for transfers between devices: 133 us -> none  [body(): shared = lax.psum(jnp.where(mine, shared, jnp.zeros_like(shared)), 'rep')]
    psum x2 -> x0, blocking collectives: 56.3 us -> none  [body(): lax.psum(jnp.stack([jnp.sum(motion * motion), jnp.sum(forces * forces)]),...]
    pallas_call x0 -> x5, Pallas kernels: none -> 37.8 us  [the longest x2 21.4 us: mix(): pl.pallas_call(functools.partial(mix_kernel, size, last), out_shape=(shap...]
    pallas_call x2, Pallas kernels: 94.8 us -> 76.5 us  [force(): pl.pallas_call(force_kernel, out_shape=jax.ShapeDtypeStruct((3, 32, 128),...]
    pallas_call x2, Pallas kernels: 45 us -> 27.2 us  [density(): pl.pallas_call(density_kernel, out_shape=jax.ShapeDtypeStruct((32, 128),...]
    ppermute x10 -> x6, waiting for transfers between devices: 11.3 us -> 0.02 us  [gather_four(): lax.ppermute(value, 'rep', [(i, i ^ stage * k) for i in range(size)])]
    ppermute x10 -> x6, starting transfers between devices: 5.11 us -> 12.3 us  [gather_four(): lax.ppermute(value, 'rep', [(i, i ^ stage * k) for i in range(size)])]
    unnamed x20 -> x36, local copies, waits for them, and re-layouts: 1.3 us -> 8.32 us
  transfers between devices with their start and end apart: 11 -> 6, of which waited for: 7 -> 0; matrix products, arithmetic and copies ran while one was open for 1% -> 0% of each run, Pallas kernels for 0% -> 41%
where the time goes in v1:
time: 170 us; the launch traced here: 167 us
  Pallas kernels  141 us (83%)
  starting transfers between devices  12.3 us (7%)
  local copies, waits for them, and re-layouts  11.4 us (7%)
    pallas_call x2, Pallas kernels, force(): pl.pallas_call(force_kernel, out_shape=jax.ShapeDtypeStruct((3, 32, 128),...  76.5 us
    pallas_call x2, Pallas kernels, density(): pl.pallas_call(density_kernel, out_shape=jax.ShapeDtypeStruct((32, 128),...  27.2 us
    pallas_call x2, Pallas kernels, mix(): pl.pallas_call(functools.partial(mix_kernel, size, last), out_shape=(shap...  21.4 us
    ppermute x6, starting transfers between devices, gather_four(): lax.ppermute(value, 'rep', [(i, i ^ stage * k) for i in range(size)])  12.3 us
    pallas_call x2, Pallas kernels, embed_halo(): pl.pallas_call(functools.partial(embed_kernel, size), out_shape=shaped(64...  10.7 us
    unnamed x36, local copies, waits for them, and re-layouts  8.32 us
    pallas_call x1, Pallas kernels, start_halo(): pl.pallas_call(functools.partial(start_kernel, size), out_shape=(shaped(3...  5.76 us
  transfers between devices with their start and end apart: 6, of which 0 were waited for; matrix products, arithmetic and copies ran while one was open for 0% of the time, Pallas kernels for 41%

profile of v1, /device:TPU:8, one launch (start us, length us, event | category | flops | bytes accessed | tf_op | source)
XLA Modules:
  0.0 167.2 jit_solution(408437481318570776)
XLA Ops:
  0.6 0.0 copy-start.15
  0.6 0.8 copy.11
  1.4 0.0 copy-done.15
  1.4 0.1 broadcast_in_dim_reshape.4
  1.5 0.6 pad.4.table_ref
  2.2 5.8 %shard_map.93 = (f32[3,64,128]{2,1,0:T(8,128)}, s32[3,16,128]{2,1,0:T(8,128)}) custom-call(f32[3,32,128]{2,1,0:T(8,128)} %bitcast.18, s32[16,128]{1,0:T(8,128)} %pad.4.table_ref), custom_call_target="tpu_custom_call" | custom-call | tf_op jit(solution)/shard_map/pallas_call | solution.py:357
  7.9 0.0 copy-start.4
  7.9 0.8 slice_bitcast_fusion.2
  8.7 0.7 slice_bitcast_fusion.1
  9.4 0.1 pad_add_fusion.flag_ref
  9.5 0.1 add_bitcast_fusion.count_ref
  9.6 0.1 lt.23
  9.7 0.0 copy-done.4
  9.7 13.6 %shard_map.94.embed_ref = f32[32,128]{1,0:T(8,128)S(1)} custom-call(f32[3,64,128]{2,1,0:T(8,128)S(1)} %copy-done.4, s32[64]{0:T(128)S(1)} %add_bitcast_fusion.count_ref, s32[13,64]{1,0:T(8,128)S(1)} %pad_add_fusion.flag_ref), custom_call_target="tpu_custom_call" | custom-call | flops 20000000000 | bytes 200000 | tf_op jit(solution)/shard_map/pallas_call | solution.py:211
  23.3 0.0 copy-start.8
  23.3 0.6 copy-done.8
  23.9 5.3 %shard_map.95.embed_ref = f32[64,128]{1,0:T(8,128)} custom-call(f32[32,128]{1,0:T(8,128)} %copy-done.8), custom_call_target="tpu_custom_call" | custom-call | tf_op jit(solution)/shard_map/pallas_call | solution.py:373
  29.2 0.0 copy-start.6
  29.3 0.7 copy-done.6
  30.0 38.2 %shard_map.96.force_ref = f32[3,32,128]{2,1,0:T(8,128)S(1)} custom-call(f32[3,64,128]{2,1,0:T(8,128)S(1)} %copy-done.4, s32[64]{0:T(128)S(1)} %add_bitcast_fusion.count_ref, s32[13,64]{1,0:T(8,128)S(1)} %pad_add_fusion.flag_ref, f32[64,128]{1,0:T(8,128)S(1)} %copy-done.6), custom_call_target="tpu_custom_call" | custom-call | flops 40000000000 | bytes 200000 | tf_op jit(solution)/shard_map/pallas_call | solution.py:223
  68.3 0.0 copy-start.1
  68.3 0.1 fusion.1
  68.3 0.7 copy-done.16
  69.0 0.0 copy-done.14
  69.0 0.0 copy-start.10
  69.1 0.0 copy-done.1
  69.1 0.8 copy-done.10
  69.9 0.6 copy-done.9
  70.5 3.0 %collective-permute-start = (f32[6,32,128]{2,1,0:T(8,128)S(1)}, f32[6,32,128]{2,1,0:T(8,128)S(1)}, u32[]{:S(2)}, u32[]{:S(2)}) collective-permute-start(f32[6,32,128]{2,1,0:T(8,128)S(1)} %maximum_select_fusion), channel_id=1, source_target_pairs={{0,16},{16,0},{32,48},{48,32},{64,80},{80,64},{96,112},{112,96},{1... | collective-permute-start | bytes 294920 | tf_op jit(solution)/shard_map/ppermute | solution.py:408
  73.5 2.0 %collective-permute-start.1 = (f32[6,32,128]{2,1,0:T(8,128)S(1)}, f32[6,32,128]{2,1,0:T(8,128)S(1)}, u32[]{:S(2)}, u32[]{:S(2)}) collective-permute-start(f32[6,32,128]{2,1,0:T(8,128)S(1)} %maximum_select_fusion), channel_id=1, source_target_pairs={{0,32},{16,48},{32,0},{48,16},{64,96},{80,112},{96,64},{112,80},{1... | collective-permute-start | bytes 294920 | tf_op jit(solution)/shard_map/ppermute | solution.py:408
  75.4 0.1 collective-permute-start.2
  75.5 11.6 %shard_map.97 = (f32[3,64,128]{2,1,0:T(8,128)}, f32[3,32,128]{2,1,0:T(8,128)}) custom-call(f32[3,32,128]{2,1,0:T(8,128)} %copy-done.9, f32[3,32,128]{2,1,0:T(8,128)} %copy-done.1, f32[3,64,128]{2,1,0:T(8,128)} %get-tuple-element.14.pos_ref.wide_ref), custom_call_target="tpu_custom_call" | custom-call | tf_op jit(solution)/shard_map/pallas_call | solution.py:389
  87.1 0.0 copy-start.2
  87.1 0.9 copy-done.2
  87.9 13.6 %shard_map.98.embed_ref = f32[32,128]{1,0:T(8,128)S(1)} custom-call(f32[3,64,128]{2,1,0:T(8,128)S(1)} %copy-done.2, s32[64]{0:T(128)S(1)} %add_bitcast_fusion.count_ref, s32[13,64]{1,0:T(8,128)S(1)} %pad_add_fusion.flag_ref), custom_call_target="tpu_custom_call" | custom-call | flops 20000000000 | bytes 200000 | tf_op jit(solution)/shard_map/pallas_call | solution.py:211
  101.5 0.0 copy-start.7
  101.5 0.1 fusion
  101.6 0.0 collective-permute-done
  101.6 0.0 collective-permute-done.1
  101.6 0.0 collective-permute-done.2
  101.7 0.5 copy-done.7
  102.1 1.9 %collective-permute-start.3 = (f32[6,32,128]{2,1,0:T(8,128)S(1)}, f32[6,32,128]{2,1,0:T(8,128)S(1)}, u32[]{:S(2)}, u32[]{:S(2)}) collective-permute-start(f32[6,32,128]{2,1,0:T(8,128)S(1)} %add_add_fusion.1), channel_id=1, source_target_pairs={{0,64},{16,80},{32,96},{48,112},{64,0},{80,16},{96,32},{112,48},{1... | collective-permute-start | bytes 294920 | tf_op jit(solution)/shard_map/ppermute | solution.py:408
  104.0 5.4 %collective-permute-start.4 = (f32[6,32,128]{2,1,0:T(8,128)S(1)}, f32[6,32,128]{2,1,0:T(8,128)S(1)}, u32[]{:S(2)}, u32[]{:S(2)}) collective-permute-start(f32[6,32,128]{2,1,0:T(8,128)S(1)} %add_add_fusion.1), channel_id=1, source_target_pairs={{0,128},{16,144},{32,160},{48,176},{64,192},{80,208},{96,224},{112... | collective-permute-start | bytes 294920 | tf_op jit(solution)/shard_map/ppermute | solution.py:408
  109.5 0.0 collective-permute-start.5
  109.5 5.3 %shard_map.99.embed_ref = f32[64,128]{1,0:T(8,128)} custom-call(f32[32,128]{1,0:T(8,128)} %copy-done.7), custom_call_target="tpu_custom_call" | custom-call | tf_op jit(solution)/shard_map/pallas_call | solution.py:373
  114.8 0.0 copy-done.3
  114.8 0.0 copy-start.5
  114.8 0.7 copy-done.5
  115.6 38.2 %shard_map.100.force_ref = f32[3,32,128]{2,1,0:T(8,128)S(1)} custom-call(f32[3,64,128]{2,1,0:T(8,128)S(1)} %copy-done.3, s32[64]{0:T(128)S(1)} %add_bitcast_fusion.count_ref, s32[13,64]{1,0:T(8,128)S(1)} %pad_add_fusion.flag_ref, f32[64,128]{1,0:T(8,128)S(1)} %copy-done.5), custom_call_target="tpu_custom_call" | custom-call | flops 40000000000 | bytes 200000 | tf_op jit(solution)/shard_map/pallas_call | solution.py:223
  153.8 0.0 copy-start
  153.8 0.0 copy-start.11
  153.8 0.0 copy-start.12
  153.8 0.0 collective-permute-done.3
  153.8 0.0 collective-permute-done.4
  153.9 0.0 collective-permute-done.5
  153.9 0.5 copy-done
  154.4 0.2 copy-done.11
  154.6 0.0 copy-done.12
  154.7 0.7 multiply_add_fusion
  155.3 9.8 %shard_map.101 = (f32[3,32,128]{2,1,0:T(8,128)}, f32[3,32,128]{2,1,0:T(8,128)}) custom-call(f32[3,32,128]{2,1,0:T(8,128)} %get-tuple-element.28.vel_ref, f32[3,32,128]{2,1,0:T(8,128)} %copy-done, f32[3,64,128]{2,1,0:T(8,128)} %get-tuple-element.17.pos_ref.wide_ref), custom_call_target="tpu_custom_call" | custom-call | tf_op jit(solution)/shard_map/pallas_call | solution.py:389
  165.1 0.0 copy-start.13
  165.1 1.4 copy.14
  166.5 0.0 copy-done.13
  166.6 0.6 copy.15
  (9 shorter events, 0.1 us)
Async XLA Ops:
  0.6 0.8 copy-start.15
  7.9 1.8 %copy-start.4 = (f32[3,64,128]{2,1,0:T(8,128)S(1)}, f32[3,64,128]{2,1,0:T(8,128)}, u32[]{:S(2)}) copy-start(f32[3,64,128]{2,1,0:T(8,128)} %get-tuple-element.14.pos_ref.wide_ref) | copy-start | bytes 294916
  23.3 0.6 copy-start.8
  29.2 0.8 copy-start.6
  30.0 39.0 %copy-start.14 = (f32[1,3,2,4,4,128]{5,4,3,2,1,0:T(4,128)S(1)}, f32[1,3,2,4,4,128]{5,4,3,2,1,0:T(4,128)}, u32[]{:S(2)}) copy-start(f32[1,3,2,4,4,128]{5,4,3,2,1,0:T(4,128)} %param.7) | copy-start | bytes 147460
  68.3 0.8 copy-start.1
  68.3 0.7 copy-start.16
  69.0 0.8 copy-start.10
  69.8 0.6 copy-start.9
  70.5 31.2 %collective-permute-start = (f32[6,32,128]{2,1,0:T(8,128)S(1)}, f32[6,32,128]{2,1,0:T(8,128)S(1)}, u32[]{:S(2)}, u32[]{:S(2)}) collective-permute-start(f32[6,32,128]{2,1,0:T(8,128)S(1)} %maximum_select_fusion), channel_id=1, source_target_pairs={{0,16},{16,0},{32,48},{48,32},{64,80},{80,64},{96,112},{112,96},{1... | collective-permute-start | bytes 294920 | tf_op jit(solution)/shard_map/ppermute | solution.py:408
  73.5 28.2 %collective-permute-start.1 = (f32[6,32,128]{2,1,0:T(8,128)S(1)}, f32[6,32,128]{2,1,0:T(8,128)S(1)}, u32[]{:S(2)}, u32[]{:S(2)}) collective-permute-start(f32[6,32,128]{2,1,0:T(8,128)S(1)} %maximum_select_fusion), channel_id=1, source_target_pairs={{0,32},{16,48},{32,0},{48,16},{64,96},{80,112},{96,64},{112,80},{1... | collective-permute-start | bytes 294920 | tf_op jit(solution)/shard_map/ppermute | solution.py:408
  75.4 26.2 %collective-permute-start.2 = (f32[6,32,128]{2,1,0:T(8,128)S(1)}, f32[6,32,128]{2,1,0:T(8,128)S(1)}, u32[]{:S(2)}, u32[]{:S(2)}) collective-permute-start(f32[6,32,128]{2,1,0:T(8,128)S(1)} %maximum_select_fusion), channel_id=1, source_target_pairs={{0,48},{16,32},{32,16},{48,0},{64,112},{80,96},{96,80},{112,64},{1... | collective-permute-start | bytes 294920 | tf_op jit(solution)/shard_map/ppermute | solution.py:408
  87.1 0.9 copy-start.2
  101.5 0.6 copy-start.7
  101.6 13.2 %copy-start.3 = (f32[3,64,128]{2,1,0:T(8,128)S(1)}, f32[3,64,128]{2,1,0:T(8,128)}, u32[]{:S(2)}) copy-start(f32[3,64,128]{2,1,0:T(8,128)} %get-tuple-element.17.pos_ref.wide_ref) | copy-start | bytes 294916
  102.1 51.7 %collective-permute-start.3 = (f32[6,32,128]{2,1,0:T(8,128)S(1)}, f32[6,32,128]{2,1,0:T(8,128)S(1)}, u32[]{:S(2)}, u32[]{:S(2)}) collective-permute-start(f32[6,32,128]{2,1,0:T(8,128)S(1)} %add_add_fusion.1), channel_id=1, source_target_pairs={{0,64},{16,80},{32,96},{48,112},{64,0},{80,16},{96,32},{112,48},{1... | collective-permute-start | bytes 294920 | tf_op jit(solution)/shard_map/ppermute | solution.py:408
  104.0 49.8 %collective-permute-start.4 = (f32[6,32,128]{2,1,0:T(8,128)S(1)}, f32[6,32,128]{2,1,0:T(8,128)S(1)}, u32[]{:S(2)}, u32[]{:S(2)}) collective-permute-start(f32[6,32,128]{2,1,0:T(8,128)S(1)} %add_add_fusion.1), channel_id=1, source_target_pairs={{0,128},{16,144},{32,160},{48,176},{64,192},{80,208},{96,224},{112... | collective-permute-start | bytes 294920 | tf_op jit(solution)/shard_map/ppermute | solution.py:408
  109.5 44.4 %collective-permute-start.5 = (f32[6,32,128]{2,1,0:T(8,128)S(1)}, f32[6,32,128]{2,1,0:T(8,128)S(1)}, u32[]{:S(2)}, u32[]{:S(2)}) collective-permute-start(f32[6,32,128]{2,1,0:T(8,128)S(1)} %add_add_fusion.1), channel_id=1, source_target_pairs={{0,192},{16,208},{32,224},{48,240},{64,128},{80,144},{96,160},{112... | collective-permute-start | bytes 294920 | tf_op jit(solution)/shard_map/ppermute | solution.py:408
  114.8 0.8 copy-start.5
  153.8 0.6 copy-start
  153.8 0.8 copy-start.11
  153.8 0.8 copy-start.12
  165.1 1.4 copy-start.13

commit v2 on v0

v2 whole, which is shorter than its diff:
```python
import functools
import math

import jax
import jax.numpy as jnp
from jax import lax
from jax.experimental import pallas as pl
from jax.experimental.pallas import tpu as pltpu
from jax.sharding import PartitionSpec as P

QUENCH = 2
STEP_SIZE = 0.1
ALPHA_MIX = 0.25
EPSILON = 1e-06
FRICTION = math.exp(-0.2)
KICK_SCALE = math.sqrt(1.0 - FRICTION * FRICTION)
HALF_OFFSETS = (
    [(1, p, q) for p in (-1, 0, 1) for q in (-1, 0, 1)]
    + [(0, 1, q) for q in (-1, 0, 1)]
    + [(0, 0, 1)]
)
OFFSETS = [(p, q, r) for p in (-1, 0, 1) for q in (-1, 0, 1) for r in (-1, 0, 1)]
FAR = -1.0e6
LEFT = (0, 1, 2, 0, 1, 0)
RIGHT = (0, 0, 0, 1, 1, 2)
DEPTH = 48
CHUNK = 128
REP_HOPS = (1, 2, 3, 4, 8, 12)
F32, BF16 = jnp.float32, jnp.bfloat16
MESH = pl.DeviceIdType.MESH


def flag_lookup(o):
    if o in HALF_OFFSETS:
        return HALF_OFFSETS.index(o), True
    return HALF_OFFSETS.index((-o[0], -o[1], -o[2])), False


def pieces(v):
    p1 = v.astype(BF16).astype(F32)
    r = v - p1
    p2 = r.astype(BF16).astype(F32)
    return p1, p2, r - p2


def split_rows(v, order):
    p = pieces(v)
    return jnp.concatenate([p[i] for i in order], axis=0)


def across(rep, hop):
    for bit in (1, 2, 4, 8):
        if hop & bit:
            rep = rep + bit - 2 * bit * lax.rem(lax.div(rep, bit), 2)
    return rep


def fold(a):
    return jnp.sum(a.reshape(a.shape[0] // 8, 8, 128), axis=0)


def squares(a):
    return jnp.sum(jnp.sum(a * a, axis=0), axis=0, keepdims=True)


def fill_constants(off_ref, pick_ref):
    row = lax.broadcasted_iota(jnp.int32, (32, 128), 0)
    third = (lax.div(row, 9) - 1, lax.rem(lax.div(row, 3), 3) - 1, lax.rem(row, 3) - 1)
    for k in range(3):
        off_ref[k] = third[k].astype(F32)
    row = lax.broadcasted_iota(jnp.int32, (DEPTH, 128), 0)
    for k in range(3):
        hit = (row == k) | (row == 8 + k) | (row == 16 + k)
        pick_ref[:, 128 * k : 128 * k + 128] = jnp.where(hit, 1.0, 0.0).astype(BF16)


def prepare_positions(pos_ref, tab_ref, left_ref, spread_ref, pick_ref):
    lane = lax.broadcasted_iota(jnp.int32, (1, 128), 1)
    ones = jnp.ones((1, 128), F32)
    zeros = jnp.zeros((3, 128), F32)

    def one(j, carry):
        live = lane < tab_ref[0, j]
        rows = [jnp.where(live, pos_ref[k, pl.ds(j, 1), :], 0.0) for k in range(3)]
        norm = jnp.where(live, -(rows[0] * rows[0] + rows[1] * rows[1] + rows[2] * rows[2]), FAR)
        v = jnp.concatenate(rows + [norm, ones, zeros], axis=0)
        left = split_rows(v, LEFT).T.astype(BF16)
        left_ref[j] = left
        spread = jnp.dot(left, pick_ref[...], preferred_element_type=F32)
        for k in range(3):
            spread_ref[j, k] = spread[:, 128 * k : 128 * k + 128]
        return carry

    lax.fori_loop(0, 64, one, 0, unroll=8)


def prepare_embed(first, count, emb_ref, left_ref):
    row = lax.broadcasted_iota(jnp.int32, (8, 128), 0)
    zeros = jnp.zeros((DEPTH - 24, 128), F32)

    def one(n, carry):
        j = first + n
        v = jnp.where(row == 5, emb_ref[pl.ds(j, 1), :], 0.0)
        table = jnp.concatenate([*pieces(v), zeros], axis=0)
        left_ref[j] = (left_ref[j].astype(F32) + table.T).astype(BF16)
        return carry

    lax.fori_loop(0, count, one, 0, unroll=8)


def centre(pos_ref, i, off_ref):
    rows = [pos_ref[k, pl.ds(i, 1), :] for k in range(3)]
    ones = jnp.ones((1, 128), F32)
    base = jnp.concatenate([2.0 * a for a in rows] + [ones, jnp.zeros((4, 128), F32)], axis=0)
    own = jnp.ones((32, 128), F32)
    for k in range(3):
        gap = rows[k] - off_ref[k]
        own = own - gap * gap
    return rows, base, own


def column(o, extra=0.0):
    row = lax.broadcasted_iota(jnp.int32, (8, 128), 0)
    col = jnp.zeros((8, 128), F32)
    for k in range(3):
        if o[k]:
            col = jnp.where(row == k, -2.0 * o[k], col)
    if extra:
        col = jnp.where(row == 5, extra, col)
    return col


def place(c, d):
    cp, cy, cz = lax.div(c, 16), lax.rem(lax.div(c, 4), 4), lax.rem(c, 4)
    return (cp + 1 + d[0]) * 16 + lax.rem(cy + d[1] + 4, 4) * 4 + lax.rem(cz + d[2] + 4, 4)


def flagged(tab_ref, i, j, o, own):
    if o == (0, 0, 0):
        return own
    h, forward = flag_lookup(o)
    flag = tab_ref[1 + h, i] if forward else tab_ref[1 + h, j]
    return jnp.where(flag > 0, own, FAR)


def not_self(t, first):
    rows = lax.broadcasted_iota(jnp.int32, t.shape, 0) + first
    cols = lax.broadcasted_iota(jnp.int32, t.shape, 1)
    return jnp.where(rows == cols, 0.0, t)


def density_pass(pos_ref, tab_ref, emb_ref, left_ref, off_ref):
    fifth = lax.broadcasted_iota(jnp.int32, (8, 128), 0) == 4

    def one(q, carry):
        c0 = 2 * q
        sets = [centre(pos_ref, c0 + 16 + k, off_ref) for k in (0, 1)]
        totals = [jnp.zeros((8, 128), F32), jnp.zeros((8, 128), F32)]
        for ox in (-1, 0, 1):
            for oy in (-1, 0, 1):
                for dz in (-1, 0, 1, 2):
                    j = place(c0, (ox, oy, dz))
                    used = [k for k in (0, 1) if -1 <= dz - k <= 1]
                    ws = []
                    for k in used:
                        o = (ox, oy, dz - k)
                        n = OFFSETS.index(o)
                        own = flagged(tab_ref, c0 + 16 + k, j, o, sets[k][2][n : n + 1])
                        ws.append(jnp.where(fifth, own, sets[k][1] + column(o)))
                    right = jnp.concatenate([split_rows(w, RIGHT) for w in ws], axis=1).astype(BF16)
                    for first in range(0, 128, CHUNK):
                        m = jnp.dot(left_ref[j, first : first + CHUNK], right, preferred_element_type=F32)
                        for n, k in enumerate(used):
                            t = jnp.maximum(m[:, 128 * n : 128 * n + 128], 0.0)
                            if (ox, oy, dz) == (0, 0, k):
                                t = not_self(t, first)
                            totals[k] = totals[k] + fold(t * t * t)
        for k in (0, 1):
            density = jnp.sum(totals[k], axis=0, keepdims=True) / 128.0
            emb_ref[pl.ds(c0 + 16 + k, 1), :] = -0.25 * lax.rsqrt(1.0 + density)
        return carry

    lax.fori_loop(0, 16, one, 0)


def force_pass(pos_ref, tab_ref, emb_ref, force_ref, left_ref, spread_ref, off_ref):
    lane = lax.broadcasted_iota(jnp.int32, (1, 128), 1)
    fifth = lax.broadcasted_iota(jnp.int32, (8, 128), 0) == 4

    def one(c, carry):
        i = c + 16
        rows, base, owns = centre(pos_ref, i, off_ref)
        e = emb_ref[pl.ds(i, 1), :]
        total = [jnp.zeros((8, 128), F32) for _ in range(3)]
        for n, o in enumerate(OFFSETS):
            j = place(c, o)
            own = flagged(tab_ref, i, j, o, owns[n : n + 1])
            w = jnp.where(fifth, own, base + column(o))
            u = jnp.where(fifth, own + e, base + column(o, 1.0))
            right = jnp.concatenate([split_rows(w, RIGHT), split_rows(u, RIGHT)], axis=1).astype(BF16)
            amount = jnp.zeros((8, 128), F32)
            for first in range(0, 128, CHUNK):
                both = jnp.dot(left_ref[j, first : first + CHUNK], right, preferred_element_type=F32)
                t = jnp.maximum(both[:, :128], 0.0)
                if o == (0, 0, 0):
                    t = not_self(t, first)
                g = t * t * both[:, 128:]
                amount = amount + fold(g)
                for k in range(3):
                    total[k] = total[k] - fold(g * spread_ref[j, k, first : first + CHUNK])
            for k in range(3):
                total[k] = total[k] + (rows[k] - o[k]) * amount
        scale = jnp.where(lane < tab_ref[0, i], 24.0 / 128.0, 0.0)
        for k in range(3):
            force_ref[k, pl.ds(c, 1), :] = jnp.sum(total[k], axis=0, keepdims=True) * scale
        return carry

    lax.fori_loop(0, 32, one, 0)


def each_row():
    for k in range(3):
        for cp in range(2):
            for cy in range(4):
                yield k, cp, cy, cp * 16 + cy * 4


def whole_kernel(
    size, pos_in, vel_in, noise_in, table_in, exit_in, qpos_out, qvel_out, dpos_out, dvel_out,
    pos, vel, frc, emb, left, spread, off, pick,
    pos_land, tab_land, emb_land, vf_land, part, slots, shared, relay, rep_land, noise, table, tab, send, recv, local,
):
    me, rep = lax.axis_index("space"), lax.axis_index("rep")
    places = [lax.rem(me + shift, size) for shift in range(1, size)]
    west, east = (rep, places[-1]), (rep, places[0])
    peers = [(rep, p) for p in places] + [(across(rep, hop), me) for hop in REP_HOPS]
    barrier = pltpu.get_barrier_semaphore()
    for where in peers:
        pl.semaphore_signal(barrier, inc=1, device_id=where, device_id_type=MESH)

    for k, cp, cy, r in each_row():
        pos[k, 16 + r : 20 + r, :] = pos_in[0, k, cp, cy]
    pl.semaphore_wait(barrier, len(peers))
    used = [0]

    def post(source, target, where):
        n = used[0]
        used[0] = n + 1
        copy = pltpu.make_async_remote_copy(
            src_ref=source,
            dst_ref=target,
            send_sem=send.at[n],
            recv_sem=recv.at[n],
            device_id=where,
            device_id_type=MESH,
        )
        copy.start()
        return copy

    flying = [
        post(table_in, tab_land.at[0], east),
        post(table_in, tab_land.at[1], west),
        post(pos.at[:, pl.ds(32, 16), :], pos_land.at[0], east),
        post(pos.at[:, pl.ds(16, 16), :], pos_land.at[1], west),
    ]
    fill_constants(off, pick)
    for k, cp, cy, r in each_row():
        vel[k, r : r + 4, :] = vel_in[0, k, cp, cy]
        noise[k, r : r + 4, :] = noise_in[0, 0, k, cp, cy]
    for copy in flying:
        copy.wait()
    lane = lax.broadcasted_iota(jnp.int32, (16, 128), 1)
    joined = jnp.where(lane < 16, pltpu.roll(tab_land[0], 112, 1), pltpu.roll(table_in[...], 16, 1))
    table[...] = jnp.where(lane < 48, joined, pltpu.roll(tab_land[1], 48, 1))
    fetch = pltpu.make_async_copy(table, tab, local.at[0])
    fetch.start()
    pos[:, 0:16, :] = pos_land[0]
    pos[:, 48:64, :] = pos_land[1]
    fetch.wait()

    lane = lax.broadcasted_iota(jnp.int32, (1, 128), 1)

    def mask_row(c, carry):
        live = lane < tab[0, c + 16]
        for k in range(3):
            vel[k, pl.ds(c, 1), :] = jnp.where(live, vel[k, pl.ds(c, 1), :], 0.0)
            noise[k, pl.ds(c, 1), :] = jnp.where(live, noise[k, pl.ds(c, 1), :], 0.0)
        return carry

    lax.fori_loop(0, 32, mask_row, 0, unroll=8)
    relays = []
    for step in range(QUENCH):
        last = step == QUENCH - 1
        prepare_positions(pos, tab, left, spread, pick)
        density_pass(pos, tab, emb, left, off)
        flying = [
            post(emb.at[pl.ds(32, 16), :], emb_land.at[step, 0], east),
            post(emb.at[pl.ds(16, 16), :], emb_land.at[step, 1], west),
        ]
        if last:
            for copy in relays:
                copy.wait()
            relay[...] = shared[...] + rep_land[0] + rep_land[1] + rep_land[2]
            relays = [post(relay, rep_land.at[n], (across(rep, REP_HOPS[n]), me)) for n in (3, 4, 5)]
        prepare_embed(16, 32, emb, left)
        for copy in flying:
            copy.wait()
        emb[0:16, :] = emb_land[step, 0]
        emb[48:64, :] = emb_land[step, 1]
        prepare_embed(0, 16, emb, left)
        prepare_embed(48, 16, emb, left)
        force_pass(pos, tab, emb, frc, left, spread, off)
        vel[...] = vel[...] + STEP_SIZE * frc[...]
        motion, forces = vel[...], frc[...]
        part[step] = jnp.concatenate([squares(motion), squares(forces), jnp.zeros((6, 128), F32)], axis=0)
        flying = [post(part.at[step], slots.at[step, n], (rep, p)) for n, p in enumerate(places)]
        if not last:
            for n, source in enumerate((vel, frc)):
                flying.append(post(source.at[:, pl.ds(16, 16), :], vf_land.at[0, n], east))
                flying.append(post(source.at[:, pl.ds(0, 16), :], vf_land.at[1, n], west))
            mine = jnp.where(rep == exit_in[0], 1.0, 0.0)
            shared[0:3] = pos[:, 16:48, :] * mine
            shared[3:6] = motion * mine
            relays = [post(shared, rep_land.at[n], (across(rep, REP_HOPS[n]), me)) for n in (0, 1, 2)]
        else:
            for copy in relays:
                copy.wait()
            totals = [relay[k] + rep_land[3, k] + rep_land[4, k] + rep_land[5, k] for k in range(6)]
            for k in range(3):
                kicked = FRICTION * totals[3 + k] + KICK_SCALE * noise[k]
                noise[k] = kicked
                shared[k] = totals[k] + STEP_SIZE * kicked
            for k, cp, cy, r in each_row():
                dvel_out[0, k, cp, cy] = noise[k, r : r + 4, :]
                dpos_out[0, k, cp, cy] = shared[k, r : r + 4, :]
        for copy in flying:
            copy.wait()
        total = part[step]
        for n in range(size - 1):
            total = total + slots[step, n]
        total = jnp.sum(total, axis=1, keepdims=True)
        mixing = (ALPHA_MIX * jnp.sqrt(total[0:1] / (total[1:2] + EPSILON)))[None]
        new = (1.0 - ALPHA_MIX) * motion + mixing * forces
        vel[...] = new
        pos[:, 16:48, :] = pos[:, 16:48, :] + STEP_SIZE * new
        if not last:
            for n, rows in enumerate((slice(0, 16), slice(48, 64))):
                moved = (1.0 - ALPHA_MIX) * vf_land[n, 0] + mixing * vf_land[n, 1]
                pos[:, rows, :] = pos[:, rows, :] + STEP_SIZE * moved
    for k, cp, cy, r in each_row():
        qpos_out[0, k, cp, cy] = pos[k, 16 + r : 20 + r, :]
        qvel_out[0, k, cp, cy] = vel[k, r : r + 4, :]


def body(positions, velocities, thermal_noise, counts, pair_flags, exit_replica):
    size = lax.axis_size("space")
    table = jnp.concatenate([counts.reshape(1, 32), pair_flags.reshape(13, 32)], axis=0)
    table = jnp.pad(table, ((0, 2), (0, 96)))
    vm = pl.BlockSpec(memory_space=pltpu.VMEM)
    sm = pl.BlockSpec(memory_space=pltpu.SMEM)
    copies = 4 + QUENCH * (2 + size - 1) + 4 + len(REP_HOPS)
    return pl.pallas_call(
        functools.partial(whole_kernel, size),
        out_shape=(jax.ShapeDtypeStruct(positions.shape, F32),) * 4,
        in_specs=[vm, vm, vm, vm, sm],
        out_specs=(vm,) * 4,
        scratch_shapes=[
            pltpu.VMEM((3, 64, 128), F32),
            pltpu.VMEM((3, 32, 128), F32),
            pltpu.VMEM((3, 32, 128), F32),
            pltpu.VMEM((64, 128), F32),
            pltpu.VMEM((64, 128, DEPTH), BF16),
            pltpu.VMEM((64, 3, 128, 128), F32),
            pltpu.VMEM((3, 32, 128), F32),
            pltpu.VMEM((DEPTH, 384), BF16),
            pltpu.VMEM((2, 3, 16, 128), F32),
            pltpu.VMEM((2, 16, 128), jnp.int32),
            pltpu.VMEM((QUENCH, 2, 16, 128), F32),
            pltpu.VMEM((2, 2, 3, 16, 128), F32),
            pltpu.VMEM((QUENCH, 8, 128), F32),
            pltpu.VMEM((QUENCH, size - 1, 8, 128), F32),
            pltpu.VMEM((6, 32, 128), F32),
            pltpu.VMEM((6, 32, 128), F32),
            pltpu.VMEM((len(REP_HOPS), 6, 32, 128), F32),
            pltpu.VMEM((3, 32, 128), F32),
            pltpu.VMEM((16, 128), jnp.int32),
            pltpu.SMEM((16, 128), jnp.int32),
            pltpu.SemaphoreType.DMA((copies,)),
            pltpu.SemaphoreType.DMA((copies,)),
            pltpu.SemaphoreType.DMA((1,)),
        ],
        compiler_params=pltpu.CompilerParams(
            collective_id=1, has_side_effects=True, vmem_limit_bytes=40 << 20
        ),
    )(positions, velocities, thermal_noise, table, exit_replica)


def solution(mesh):
    atoms = P("rep", None, "space", None, None, None)
    placed = (
        atoms,
        atoms,
        P("rep", None, None, "space", None, None, None),
        P("space", None, None),
        P(None, "space", None, None),
        P(),
    )
    return jax.shard_map(body, mesh=mesh, in_specs=placed, out_specs=(atoms,) * 4, check_vma=False)
```

time: 380 us -> 134 us (0.35)
  waiting for transfers between devices: 144 us -> 0 us
  blocking collectives: 56.3 us -> 0 us
  between operations: 16.9 us -> 0.68 us
  Pallas kernels: 140 us -> 125 us
  other arithmetic: 12.5 us -> 0.01 us
  starting transfers between devices: 5.14 us -> 0 us
    psum x1 -> x0, waiting for transfers between devices: 133 us -> none  [body(): shared = lax.psum(jnp.where(mine, shared, jnp.zeros_like(shared)), 'rep')]
    psum x2 -> x0, blocking collectives: 56.3 us -> none  [body(): lax.psum(jnp.stack([jnp.sum(motion * motion), jnp.sum(forces * forces)]),...]
    pallas_call x4 -> x1, Pallas kernels: 140 us -> 125 us  [body(): pl.pallas_call(functools.partial(whole_kernel, size), out_shape=(jax.Shap...]
    ppermute x10 -> x0, waiting for transfers between devices: 11.3 us -> none  [the longest x5 9.25 us: widen(): lax.ppermute(lax.slice_in_dim(block, half, None, axis=dim), 'space', forw...]
    ppermute x10 -> x0, starting transfers between devices: 5.11 us -> none  [the longest x5 4.07 us: widen(): lax.ppermute(lax.slice_in_dim(block, 0, half, axis=dim), 'space', backward)]
  transfers between devices with their start and end apart: 11 -> 0, of which waited for: 7 -> 0; matrix products, arithmetic and copies ran while one was open for 1% -> 0% of each run, Pallas kernels for 0% -> 0%
where the time goes in v2:
time: 134 us; the launch traced here: 132 us
  Pallas kernels  125 us (93%)
  local copies, waits for them, and re-layouts  6.3 us (5%)
    pallas_call x1, Pallas kernels, body(): pl.pallas_call(functools.partial(whole_kernel, size), out_shape=(jax.Shap...  125 us
    unnamed x12, local copies, waits for them, and re-layouts  4.71 us

profile of v2, /device:TPU:8, one launch (start us, length us, event | category | flops | bytes accessed | tf_op | source)
XLA Modules:
  0.0 131.9 jit_solution(4377110060511131333)
XLA Ops:
  0.6 0.0 copy-start
  0.6 0.8 reshape.14
  1.4 0.8 copy.11
  2.2 0.0 copy-start.3
  2.3 0.0 copy-done
  2.3 0.6 copy-done.3
  2.9 0.0 copy-start.1
  2.9 0.8 copy-done.1
  3.7 0.0 copy-start.2
  3.7 0.8 copy-done.2
  4.5 124.9 %shard_map.93 = (f32[1,3,2,4,4,128]{5,4,3,2,1,0:T(4,128)S(1)}, f32[1,3,2,4,4,128]{5,4,3,2,1,0:T(4,128)S(1)}, f32[1,3,2,4,4,128]{5,4,3,2,1,0:T(4,128)S(1)}, f32[1,3,2,4,4,128]{5,4,3,2,1,0:T(4,128)S(1)}) custom-call(f32[1,3,2,4,4,128]{5,4,3,2,1,0:T(4,128)S(1)} %copy-done, f32[1,3,2,4,4,128]{5,4,3,2,1,0:T(4,128)S(1)} %copy-done.1, ...), custom_call_target="tpu_custom_call" | custom-call | tf_op jit(solution)/shard_map/pallas_call | solution.py:362
  129.4 0.6 copy.16
  130.0 0.6 copy.17
  130.7 0.6 copy.18
  131.3 0.6 copy.19
  (2 shorter events, 0.0 us)
Async XLA Ops:
  0.6 1.6 %copy-start = (f32[1,3,2,4,4,128]{5,4,3,2,1,0:T(4,128)S(1)}, f32[1,3,2,4,4,128]{5,4,3,2,1,0:T(4,128)}, u32[]{:S(2)}) copy-start(f32[1,3,2,4,4,128]{5,4,3,2,1,0:T(4,128)} %pos_in.1) | copy-start | bytes 147460
  2.2 0.7 copy-start.3
  2.9 0.8 copy-start.1
  3.7 0.8 copy-start.2

commit v3 on v2

--- a/solution.py
+++ b/solution.py
@@ -24,7 +24,8 @@
 LEFT = (0, 1, 2, 0, 1, 0)
 RIGHT = (0, 0, 0, 1, 1, 2)
 DEPTH = 48
-CHUNK = 128
+DENSITY_CELLS = 4
+FORCE_CELLS = 2
 REP_HOPS = (1, 2, 3, 4, 8, 12)
 F32, BF16 = jnp.float32, jnp.bfloat16
 MESH = pl.DeviceIdType.MESH
@@ -108,26 +109,50 @@
     lax.fori_loop(0, count, one, 0, unroll=8)
 
 
-def centre(pos_ref, i, off_ref):
+def centre(pos_ref, i, off_ref, own_ref, slot, e=None):
     rows = [pos_ref[k, pl.ds(i, 1), :] for k in range(3)]
     ones = jnp.ones((1, 128), F32)
-    base = jnp.concatenate([2.0 * a for a in rows] + [ones, jnp.zeros((4, 128), F32)], axis=0)
+    zeros = jnp.zeros((4, 128), F32)
+    shifted = {
+        v: pieces(jnp.concatenate([2.0 * (a - v) for a in rows] + [ones, zeros], axis=0)) for v in (-1, 0, 1)
+    }
     own = jnp.ones((32, 128), F32)
     for k in range(3):
         gap = rows[k] - off_ref[k]
         own = own - gap * gap
-    return rows, base, own
-
-
-def column(o, extra=0.0):
+    for k, part in enumerate(pieces(own)):
+        own_ref[slot, k] = part
+    if e is not None:
+        for k, part in enumerate(pieces(own + e)):
+            own_ref[slot, 3 + k] = part
+    return rows, shifted
+
+
+def row_masks():
     row = lax.broadcasted_iota(jnp.int32, (8, 128), 0)
-    col = jnp.zeros((8, 128), F32)
-    for k in range(3):
-        if o[k]:
-            col = jnp.where(row == k, -2.0 * o[k], col)
-    if extra:
-        col = jnp.where(row == 5, extra, col)
-    return col
+    return row == 0, row < 2, row == 4
+
+
+def in_plane(shifted, ox, oy, masks):
+    return [jnp.where(masks[0], shifted[ox][k], shifted[oy][k]) for k in range(3)]
+
+
+def order_rows(parts):
+    return jnp.concatenate([parts[i] for i in RIGHT], axis=0).astype(BF16)
+
+
+def right_rows(flat, shifted, o, live, own_ref, slot, masks, second=None):
+    n = OFFSETS.index(o)
+    parts = [jnp.where(masks[1], flat[k], shifted[o[2]][k]) for k in range(3)]
+    own = [own_ref[slot, k, n : n + 1] for k in range(3)]
+    if live is not None:
+        own[0] = jnp.where(live, own[0], FAR)
+    plain = order_rows([jnp.where(masks[2], own[k], parts[k]) for k in range(3)])
+    if second is None:
+        return plain
+    parts[0] = parts[0] + second
+    both = order_rows([jnp.where(masks[2], own_ref[slot, 3 + k, n : n + 1], parts[k]) for k in range(3)])
+    return jnp.concatenate([plain, both], axis=1)
 
 
 def place(c, d):
@@ -135,12 +160,11 @@
     return (cp + 1 + d[0]) * 16 + lax.rem(cy + d[1] + 4, 4) * 4 + lax.rem(cz + d[2] + 4, 4)
 
 
-def flagged(tab_ref, i, j, o, own):
+def listed(tab_ref, i, j, o):
     if o == (0, 0, 0):
-        return own
+        return None
     h, forward = flag_lookup(o)
-    flag = tab_ref[1 + h, i] if forward else tab_ref[1 + h, j]
-    return jnp.where(flag > 0, own, FAR)
+    return (tab_ref[1 + h, i] if forward else tab_ref[1 + h, j]) > 0
 
 
 def not_self(t, first):
@@ -149,73 +173,97 @@
     return jnp.where(rows == cols, 0.0, t)
 
 
-def density_pass(pos_ref, tab_ref, emb_ref, left_ref, off_ref):
-    fifth = lax.broadcasted_iota(jnp.int32, (8, 128), 0) == 4
+def walk(width):
+    for ox in (-1, 0, 1):
+        for oy in (-1, 0, 1):
+            for dz in range(-1, width + 1) if width < 4 else range(4):
+                used = []
+                for k in range(width):
+                    oz = dz - k
+                    if width == 4 and abs(oz) == 3:
+                        oz = -oz // 3
+                    if -1 <= oz <= 1:
+                        used.append((k, (ox, oy, oz)))
+                yield ox, oy, dz, used
+
+
+def density_pass(pos_ref, tab_ref, emb_ref, left_ref, off_ref, own_ref):
+    masks = row_masks()
+    width = DENSITY_CELLS
 
     def one(q, carry):
-        c0 = 2 * q
-        sets = [centre(pos_ref, c0 + 16 + k, off_ref) for k in (0, 1)]
-        totals = [jnp.zeros((8, 128), F32), jnp.zeros((8, 128), F32)]
-        for ox in (-1, 0, 1):
-            for oy in (-1, 0, 1):
-                for dz in (-1, 0, 1, 2):
-                    j = place(c0, (ox, oy, dz))
-                    used = [k for k in (0, 1) if -1 <= dz - k <= 1]
-                    ws = []
-                    for k in used:
-                        o = (ox, oy, dz - k)
-                        n = OFFSETS.index(o)
-                        own = flagged(tab_ref, c0 + 16 + k, j, o, sets[k][2][n : n + 1])
-                        ws.append(jnp.where(fifth, own, sets[k][1] + column(o)))
-                    right = jnp.concatenate([split_rows(w, RIGHT) for w in ws], axis=1).astype(BF16)
-                    for first in range(0, 128, CHUNK):
-                        m = jnp.dot(left_ref[j, first : first + CHUNK], right, preferred_element_type=F32)
-                        for n, k in enumerate(used):
-                            t = jnp.maximum(m[:, 128 * n : 128 * n + 128], 0.0)
-                            if (ox, oy, dz) == (0, 0, k):
-                                t = not_self(t, first)
-                            totals[k] = totals[k] + fold(t * t * t)
-        for k in (0, 1):
+        c0 = width * q
+        sets = [centre(pos_ref, c0 + 16 + k, off_ref, own_ref, k) for k in range(width)]
+        totals = [jnp.zeros((8, 128), F32)] * width
+        flats = None
+        for ox, oy, dz, used in walk(width):
+            if dz in (-1, 0) and used[0][1][2] == (dz if width < 4 else 0):
+                flats = [in_plane(s[1], ox, oy, masks) for s in sets]
+            j = place(c0, (ox, oy, dz))
+            right = [
+                right_rows(flats[k], sets[k][1], o, listed(tab_ref, c0 + 16 + k, j, o), own_ref, k, masks)
+                for k, o in used
+            ]
+            m = jnp.dot(left_ref[j], jnp.concatenate(right, axis=1), preferred_element_type=F32)
+            for first in range(0, 128, 8):
+                for n, (k, o) in enumerate(used):
+                    t = jnp.maximum(m[first : first + 8, 128 * n : 128 * n + 128], 0.0)
+                    if o == (0, 0, 0):
+                        t = not_self(t, first)
+                    totals[k] = totals[k] + t * t * t
+        for k in range(width):
             density = jnp.sum(totals[k], axis=0, keepdims=True) / 128.0
             emb_ref[pl.ds(c0 + 16 + k, 1), :] = -0.25 * lax.rsqrt(1.0 + density)
         return carry
 
-    lax.fori_loop(0, 16, one, 0)
-
-
-def force_pass(pos_ref, tab_ref, emb_ref, force_ref, left_ref, spread_ref, off_ref):
+    lax.fori_loop(0, 32 // width, one, 0)
+
+
+def force_pass(pos_ref, tab_ref, emb_ref, force_ref, left_ref, spread_ref, off_ref, own_ref):
     lane = lax.broadcasted_iota(jnp.int32, (1, 128), 1)
-    fifth = lax.broadcasted_iota(jnp.int32, (8, 128), 0) == 4
-
-    def one(c, carry):
-        i = c + 16
-        rows, base, owns = centre(pos_ref, i, off_ref)
-        e = emb_ref[pl.ds(i, 1), :]
-        total = [jnp.zeros((8, 128), F32) for _ in range(3)]
-        for n, o in enumerate(OFFSETS):
-            j = place(c, o)
-            own = flagged(tab_ref, i, j, o, owns[n : n + 1])
-            w = jnp.where(fifth, own, base + column(o))
-            u = jnp.where(fifth, own + e, base + column(o, 1.0))
-            right = jnp.concatenate([split_rows(w, RIGHT), split_rows(u, RIGHT)], axis=1).astype(BF16)
-            amount = jnp.zeros((8, 128), F32)
-            for first in range(0, 128, CHUNK):
-                both = jnp.dot(left_ref[j, first : first + CHUNK], right, preferred_element_type=F32)
-                t = jnp.maximum(both[:, :128], 0.0)
-                if o == (0, 0, 0):
-                    t = not_self(t, first)
-                g = t * t * both[:, 128:]
-                amount = amount + fold(g)
-                for k in range(3):
-                    total[k] = total[k] - fold(g * spread_ref[j, k, first : first + CHUNK])
-            for k in range(3):
-                total[k] = total[k] + (rows[k] - o[k]) * amount
-        scale = jnp.where(lane < tab_ref[0, i], 24.0 / 128.0, 0.0)
-        for k in range(3):
-            force_ref[k, pl.ds(c, 1), :] = jnp.sum(total[k], axis=0, keepdims=True) * scale
+    second = jnp.where(lax.broadcasted_iota(jnp.int32, (8, 128), 0) == 5, 1.0, 0.0)
+    masks = row_masks()
+    width = FORCE_CELLS
+
+    def one(q, carry):
+        c0 = width * q
+        sets = [
+            centre(pos_ref, c0 + 16 + k, off_ref, own_ref, k, emb_ref[pl.ds(c0 + 16 + k, 1), :])
+            for k in range(width)
+        ]
+        total = [[jnp.zeros((8, 128), F32) for _ in range(3)] for _ in range(width)]
+        flats = None
+        for ox, oy, dz, used in walk(width):
+            if dz in (-1, 0) and used[0][1][2] == (dz if width < 4 else 0):
+                flats = [in_plane(s[1], ox, oy, masks) for s in sets]
+            j = place(c0, (ox, oy, dz))
+            boths, amounts = [], []
+            for k, o in used:
+                right = right_rows(
+                    flats[k], sets[k][1], o, listed(tab_ref, c0 + 16 + k, j, o), own_ref, k, masks, second
+                )
+                boths.append(jnp.dot(left_ref[j], right, preferred_element_type=F32))
+                amounts.append(jnp.zeros((8, 128), F32))
+            for first in range(0, 128, 8):
+                spread = [spread_ref[j, d, first : first + 8] for d in range(3)]
+                for n, (k, o) in enumerate(used):
+                    t = jnp.maximum(boths[n][first : first + 8, :128], 0.0)
+                    if o == (0, 0, 0):
+                        t = not_self(t, first)
+                    g = t * t * boths[n][first : first + 8, 128:]
+                    amounts[n] = amounts[n] + g
+                    for d in range(3):
+                        total[k][d] = total[k][d] - g * spread[d]
+            for n, (k, o) in enumerate(used):
+                for d in range(3):
+                    total[k][d] = total[k][d] + (sets[k][0][d] - o[d]) * amounts[n]
+        for k in range(width):
+            scale = jnp.where(lane < tab_ref[0, c0 + 16 + k], 24.0 / 128.0, 0.0)
+            for d in range(3):
+                force_ref[d, pl.ds(c0 + k, 1), :] = jnp.sum(total[k][d], axis=0, keepdims=True) * scale
         return carry
 
-    lax.fori_loop(0, 32, one, 0)
+    lax.fori_loop(0, 32 // width, one, 0)
 
 
 def each_row():
@@ -226,9 +274,9 @@
 
 
 def whole_kernel(
-    size, pos_in, vel_in, noise_in, table_in, exit_in, qpos_out, qvel_out, dpos_out, dvel_out,
-    pos, vel, frc, emb, left, spread, off, pick,
-    pos_land, tab_land, emb_land, vf_land, part, slots, shared, relay, rep_land, noise, table, tab, send, recv, local,
+    size, pos_in, vel_in, table_in, exit_in, pos_out, vel_out, frc_out, xpos_out, xvel_out, occ_out, mix_out,
+    pos, vel, frc, emb, left, spread, off, own, pick,
+    pos_land, tab_land, emb_land, vf_land, part, slots, shared, relay, rep_land, pos_copy, vel_copy, occ, table, tab, send, recv, local,
 ):
     me, rep = lax.axis_index("space"), lax.axis_index("rep")
     places = [lax.rem(me + shift, size) for shift in range(1, size)]
@@ -238,8 +286,18 @@
     for where in peers:
         pl.semaphore_signal(barrier, inc=1, device_id=where, device_id_type=MESH)
 
+    loads = [
+        pltpu.make_async_copy(source.at[0], target, local.at[1 + n])
+        for n, (source, target) in enumerate(((pos_in, pos_copy), (vel_in, vel_copy)))
+    ]
+    for load in loads:
+        load.start()
+    fill_constants(off, pick)
+    for load in loads:
+        load.wait()
     for k, cp, cy, r in each_row():
-        pos[k, 16 + r : 20 + r, :] = pos_in[0, k, cp, cy]
+        pos[k, 16 + r : 20 + r, :] = pos_copy[k, cp, cy]
+        vel[k, r : r + 4, :] = vel_copy[k, cp, cy]
     pl.semaphore_wait(barrier, len(peers))
     used = [0]
 
@@ -263,10 +321,6 @@
         post(pos.at[:, pl.ds(32, 16), :], pos_land.at[0], east),
         post(pos.at[:, pl.ds(16, 16), :], pos_land.at[1], west),
     ]
-    fill_constants(off, pick)
-    for k, cp, cy, r in each_row():
-        vel[k, r : r + 4, :] = vel_in[0, k, cp, cy]
-        noise[k, r : r + 4, :] = noise_in[0, 0, k, cp, cy]
     for copy in flying:
         copy.wait()
     lane = lax.broadcasted_iota(jnp.int32, (16, 128), 1)
@@ -282,9 +336,9 @@
 
     def mask_row(c, carry):
         live = lane < tab[0, c + 16]
+        occ[pl.ds(c, 1), :] = jnp.where(live, KICK_SCALE, 0.0)
         for k in range(3):
             vel[k, pl.ds(c, 1), :] = jnp.where(live, vel[k, pl.ds(c, 1), :], 0.0)
-            noise[k, pl.ds(c, 1), :] = jnp.where(live, noise[k, pl.ds(c, 1), :], 0.0)
         return carry
 
     lax.fori_loop(0, 32, mask_row, 0, unroll=8)
@@ -292,7 +346,7 @@
     for step in range(QUENCH):
         last = step == QUENCH - 1
         prepare_positions(pos, tab, left, spread, pick)
-        density_pass(pos, tab, emb, left, off)
+        density_pass(pos, tab, emb, left, off, own)
         flying = [
             post(emb.at[pl.ds(32, 16), :], emb_land.at[step, 0], east),
             post(emb.at[pl.ds(16, 16), :], emb_land.at[step, 1], west),
@@ -309,7 +363,7 @@
         emb[48:64, :] = emb_land[step, 1]
         prepare_embed(0, 16, emb, left)
         prepare_embed(48, 16, emb, left)
-        force_pass(pos, tab, emb, frc, left, spread, off)
+        force_pass(pos, tab, emb, frc, left, spread, off, own)
         vel[...] = vel[...] + STEP_SIZE * frc[...]
         motion, forces = vel[...], frc[...]
         part[step] = jnp.concatenate([squares(motion), squares(forces), jnp.zeros((6, 128), F32)], axis=0)
@@ -325,31 +379,33 @@
         else:
             for copy in relays:
                 copy.wait()
-            totals = [relay[k] + rep_land[3, k] + rep_land[4, k] + rep_land[5, k] for k in range(6)]
-            for k in range(3):
-                kicked = FRICTION * totals[3 + k] + KICK_SCALE * noise[k]
-                noise[k] = kicked
-                shared[k] = totals[k] + STEP_SIZE * kicked
+            for n in range(6):
+                shared[n] = relay[n] + rep_land[3, n] + rep_land[4, n] + rep_land[5, n]
             for k, cp, cy, r in each_row():
-                dvel_out[0, k, cp, cy] = noise[k, r : r + 4, :]
-                dpos_out[0, k, cp, cy] = shared[k, r : r + 4, :]
+                pos_out[0, k, cp, cy] = pos[k, 16 + r : 20 + r, :]
+                vel_out[0, k, cp, cy] = vel[k, r : r + 4, :]
+                frc_out[0, k, cp, cy] = frc[k, r : r + 4, :]
+                xpos_out[0, k, cp, cy] = shared[k, r : r + 4, :]
+                xvel_out[0, k, cp, cy] = shared[3 + k, r : r + 4, :]
+                if k == 0:
+                    occ_out[cp, cy] = occ[r : r + 4, :]
         for copy in flying:
             copy.wait()
         total = part[step]
         for n in range(size - 1):
             total = total + slots[step, n]
         total = jnp.sum(total, axis=1, keepdims=True)
-        mixing = (ALPHA_MIX * jnp.sqrt(total[0:1] / (total[1:2] + EPSILON)))[None]
-        new = (1.0 - ALPHA_MIX) * motion + mixing * forces
-        vel[...] = new
-        pos[:, 16:48, :] = pos[:, 16:48, :] + STEP_SIZE * new
-        if not last:
+        mixing = ALPHA_MIX * jnp.sqrt(total[0:1] / (total[1:2] + EPSILON))
+        if last:
+            mix_out[...] = jnp.broadcast_to(mixing, (1, 128))
+        else:
+            mixing = mixing[None]
+            new = (1.0 - ALPHA_MIX) * motion + mixing * forces
+            vel[...] = new
+            pos[:, 16:48, :] = pos[:, 16:48, :] + STEP_SIZE * new
             for n, rows in enumerate((slice(0, 16), slice(48, 64))):
                 moved = (1.0 - ALPHA_MIX) * vf_land[n, 0] + mixing * vf_land[n, 1]
                 pos[:, rows, :] = pos[:, rows, :] + STEP_SIZE * moved
-    for k, cp, cy, r in each_row():
-        qpos_out[0, k, cp, cy] = pos[k, 16 + r : 20 + r, :]
-        qvel_out[0, k, cp, cy] = vel[k, r : r + 4, :]
 
 
 def body(positions, velocities, thermal_noise, counts, pair_flags, exit_replica):
@@ -359,11 +415,14 @@
     vm = pl.BlockSpec(memory_space=pltpu.VMEM)
     sm = pl.BlockSpec(memory_space=pltpu.SMEM)
     copies = 4 + QUENCH * (2 + size - 1) + 4 + len(REP_HOPS)
-    return pl.pallas_call(
+    pos, vel, frc, xpos, xvel, kick, mixing = pl.pallas_call(
         functools.partial(whole_kernel, size),
-        out_shape=(jax.ShapeDtypeStruct(positions.shape, F32),) * 4,
-        in_specs=[vm, vm, vm, vm, sm],
-        out_specs=(vm,) * 4,
+        out_shape=(jax.ShapeDtypeStruct(positions.shape, F32),) * 5 + (
+            jax.ShapeDtypeStruct((2, 4, 4, 128), F32),
+            jax.ShapeDtypeStruct((1, 128), F32),
+        ),
+        in_specs=[pl.BlockSpec(memory_space=pltpu.HBM)] * 2 + [vm, sm],
+        out_specs=(vm,) * 7,
         scratch_shapes=[
             pltpu.VMEM((3, 64, 128), F32),
             pltpu.VMEM((3, 32, 128), F32),
@@ -372,6 +431,7 @@
             pltpu.VMEM((64, 128, DEPTH), BF16),
             pltpu.VMEM((64, 3, 128, 128), F32),
             pltpu.VMEM((3, 32, 128), F32),
+            pltpu.VMEM((4, 6, 32, 128), F32),
             pltpu.VMEM((DEPTH, 384), BF16),
             pltpu.VMEM((2, 3, 16, 128), F32),
             pltpu.VMEM((2, 16, 128), jnp.int32),
@@ -382,17 +442,22 @@
             pltpu.VMEM((6, 32, 128), F32),
             pltpu.VMEM((6, 32, 128), F32),
             pltpu.VMEM((len(REP_HOPS), 6, 32, 128), F32),
-            pltpu.VMEM((3, 32, 128), F32),
+            pltpu.VMEM((3, 2, 4, 4, 128), F32),
+            pltpu.VMEM((3, 2, 4, 4, 128), F32),
+            pltpu.VMEM((32, 128), F32),
             pltpu.VMEM((16, 128), jnp.int32),
             pltpu.SMEM((16, 128), jnp.int32),
             pltpu.SemaphoreType.DMA((copies,)),
             pltpu.SemaphoreType.DMA((copies,)),
-            pltpu.SemaphoreType.DMA((1,)),
+            pltpu.SemaphoreType.DMA((3,)),
         ],
         compiler_params=pltpu.CompilerParams(
             collective_id=1, has_side_effects=True, vmem_limit_bytes=40 << 20
         ),
-    )(positions, velocities, thermal_noise, table, exit_replica)
+    )(positions, velocities, table, exit_replica)
+    quench_vel = (1.0 - ALPHA_MIX) * vel + mixing.reshape(128) * frc
+    dephase_vel = FRICTION * xvel + kick * thermal_noise[0]
+    return pos + STEP_SIZE * quench_vel, quench_vel, xpos + STEP_SIZE * dephase_vel, dephase_vel
 
 
 def solution(mesh):

time: 134 us -> 123 us (0.918)
  Pallas kernels: 125 us -> 117 us
  local copies, waits for them, and re-layouts: 6.3 us -> 3.02 us
    pallas_call x1, Pallas kernels: 125 us -> 117 us  [body(): pl.pallas_call(functools.partial(whole_kernel, size), out_shape=(jax.Shap...]
    unnamed x12 -> x8, local copies, waits for them, and re-layouts: 4.71 us -> 1.43 us
where the time goes in v3:
time: 123 us; the launch traced here: 121 us
  Pallas kernels  117 us (95%)
  local copies, waits for them, and re-layouts  3.02 us (2%)
    pallas_call x1, Pallas kernels, body(): pl.pallas_call(functools.partial(whole_kernel, size), out_shape=(jax.Shap...  117 us

profile of v3, /device:TPU:8, one launch (start us, length us, event | category | flops | bytes accessed | tf_op | source)
XLA Modules:
  0.0 121.1 jit_solution(11972934990717082881)
XLA Ops:
  0.6 0.0 copy-start
  0.6 0.8 reshape.32
  1.4 0.8 copy.11
  2.2 0.0 copy-start.2
  2.3 0.0 copy-done
  2.3 0.6 copy-done.2
  2.9 0.0 copy-start.1
  2.9 0.8 copy-done.1
  3.7 0.0 copy-start.3
  3.7 116.7 %shard_map.93 = (f32[1,3,2,4,4,128]{5,4,3,2,1,0:T(4,128)S(1)}, f32[1,3,2,4,4,128]{5,4,3,2,1,0:T(4,128)S(1)}, f32[1,3,2,4,4,128]{5,4,3,2,1,0:T(4,128)S(1)}, f32[1...) custom-call(f32[1,3,2,4,4,128]{5,4,3,2,1,0:T(4,128)S(1)} %copy-done,, ...), custom_call_target="tpu_custom_call" | custom-call | tf_op jit(solution)/shard_map/pallas_call | solution.py:418
  120.4 0.0 copy-done.3
  120.4 0.7 multiply_add_fusion
  (2 shorter events, 0.0 us)
Async XLA Ops:
  0.6 1.6 %copy-start = (f32[1,3,2,4,4,128]{5,4,3,2,1,0:T(4,128)S(1)}, f32[1,3,2,4,4,128]{5,4,3,2,1,0:T(4,128)}, u32[]{:S(2)}) copy-start(f32[1,3,2,4,4,128]{5,4,3,2,1,0:T(4,128)} %pos_in.1) | copy-start | bytes 147460
  2.2 0.7 copy-start.2
  2.9 0.8 copy-start.1
  3.7 116.7 %copy-start.3 = (f32[1,1,3,2,4,4,128]{6,5,4,3,2,1,0:T(4,128)S(1)}, f32[1,1,3,2,4,4,128]{6,5,4,3,2,1,0:T(4,128)}, u32[]{:S(2)}) copy-start(f32[1,1,3,2,4,4,128]{6,5,4,3,2,1,0:T(4,128)} %param.8) | copy-start | bytes 147460

commit v4 on v3

--- a/solution.py
+++ b/solution.py
@@ -276,7 +276,7 @@
 def whole_kernel(
     size, pos_in, vel_in, table_in, exit_in, pos_out, vel_out, frc_out, xpos_out, xvel_out, occ_out, mix_out,
     pos, vel, frc, emb, left, spread, off, own, pick,
-    pos_land, tab_land, emb_land, vf_land, part, slots, shared, relay, rep_land, pos_copy, vel_copy, occ, table, tab, send, recv, local,
+    pos_land, tab_land, emb_land, vf_land, part, slots, shared, relay, rep_land, pos_copy, vel_copy, occ, listing, table, tab, send, recv, local,
 ):
     me, rep = lax.axis_index("space"), lax.axis_index("rep")
     places = [lax.rem(me + shift, size) for shift in range(1, size)]
@@ -293,6 +293,9 @@
     for load in loads:
         load.start()
     fill_constants(off, pick)
+    stack = jnp.concatenate([table_in[cp, cy] for cp in range(2) for cy in range(4)], axis=0).astype(F32)
+    stack = jnp.concatenate([stack, jnp.zeros((96, 128), F32)], axis=0).T
+    listing[...] = stack[:16].astype(jnp.int32)
     for load in loads:
         load.wait()
     for k, cp, cy, r in each_row():
@@ -316,15 +319,15 @@
         return copy
 
     flying = [
-        post(table_in, tab_land.at[0], east),
-        post(table_in, tab_land.at[1], west),
+        post(listing, tab_land.at[0], east),
+        post(listing, tab_land.at[1], west),
         post(pos.at[:, pl.ds(32, 16), :], pos_land.at[0], east),
         post(pos.at[:, pl.ds(16, 16), :], pos_land.at[1], west),
     ]
     for copy in flying:
         copy.wait()
     lane = lax.broadcasted_iota(jnp.int32, (16, 128), 1)
-    joined = jnp.where(lane < 16, pltpu.roll(tab_land[0], 112, 1), pltpu.roll(table_in[...], 16, 1))
+    joined = jnp.where(lane < 16, pltpu.roll(tab_land[0], 112, 1), pltpu.roll(listing[...], 16, 1))
     table[...] = jnp.where(lane < 48, joined, pltpu.roll(tab_land[1], 48, 1))
     fetch = pltpu.make_async_copy(table, tab, local.at[0])
     fetch.start()
@@ -410,8 +413,9 @@
 
 def body(positions, velocities, thermal_noise, counts, pair_flags, exit_replica):
     size = lax.axis_size("space")
-    table = jnp.concatenate([counts.reshape(1, 32), pair_flags.reshape(13, 32)], axis=0)
-    table = jnp.pad(table, ((0, 2), (0, 96)))
+    table = jnp.pad(pair_flags.transpose(1, 2, 3, 0), ((0, 0),) * 3 + ((1, 114),))
+    first = lax.broadcasted_iota(jnp.int32, table.shape, 3) == 0
+    table = jnp.where(first, counts[..., None], table)
     vm = pl.BlockSpec(memory_space=pltpu.VMEM)
     sm = pl.BlockSpec(memory_space=pltpu.SMEM)
     copies = 4 + QUENCH * (2 + size - 1) + 4 + len(REP_HOPS)
@@ -446,13 +450,14 @@
             pltpu.VMEM((3, 2, 4, 4, 128), F32),
             pltpu.VMEM((32, 128), F32),
             pltpu.VMEM((16, 128), jnp.int32),
+            pltpu.VMEM((16, 128), jnp.int32),
             pltpu.SMEM((16, 128), jnp.int32),
             pltpu.SemaphoreType.DMA((copies,)),
             pltpu.SemaphoreType.DMA((copies,)),
             pltpu.SemaphoreType.DMA((3,)),
         ],
         compiler_params=pltpu.CompilerParams(
-            collective_id=1, has_side_effects=True, vmem_limit_bytes=40 << 20
+            collective_id=1, has_side_effects=True, vmem_limit_bytes=58 << 20
         ),
     )(positions, velocities, table, exit_replica)
     quench_vel = (1.0 - ALPHA_MIX) * vel + mixing.reshape(128) * frc

time: 123 us -> 125 us (1.016)
  local copies, waits for them, and re-layouts: 3.02 us -> 0.66 us
  other arithmetic: 0.72 us -> 3.04 us
    reshape x2 -> x0, local copies, waits for them, and re-layouts: 1.58 us -> none  [the longest x1 0.8 us: body(): pair_flags.reshape(13, 32)]
    pallas_call x1, Pallas kernels: 117 us -> 118 us  [body(): pl.pallas_call(functools.partial(whole_kernel, size), out_shape=(jax.Shap...]
    select_n x0 -> x1, other arithmetic: none -> 1.41 us  [body(): table = jnp.where(first, counts[..., None], table)]
where the time goes in v4:
time: 125 us; the launch traced here: 123 us
  Pallas kernels  118 us (94%)
  other arithmetic  3.04 us (2%)
    pallas_call x1, Pallas kernels, body(): pl.pallas_call(functools.partial(whole_kernel, size), out_shape=(jax.Shap...  118 us

profile of v4, /device:TPU:8, one launch (start us, length us, event | category | flops | bytes accessed | tf_op | source)
XLA Modules:
  0.0 122.5 jit_solution(1364080953385606345)
XLA Ops:
  0.6 1.4 %pad_select_fusion.table_in = s32[2,4,4,128]{3,2,1,0:T(4,128)} fusion(s32[2,4,4,13]{3,2,1,0:T(4,128)} %bitcast.7, s32[2,4,4]{2,1,0:T(4,128)} %param.9, pred[128]{0:T(512)(128)(4,1)S(1)} %iota_compare_fusion), kind=kLoop, calls=%fused_computation.5 | loop fusion | flops 4096 | bytes 18304 | tf_op jit(solution)/shard_map/jit(_where)/select_n | solution.py:418
  2.1 0.0 copy-start
  2.1 118.2 %shard_map.93 = (f32[1,3,2,4,4,128]{5,4,3,2,1,0:T(4,128)}, f32[1,3,2,4,4,128]{5,4,3,2,1,0:T(4,128)}, f32[1,3,2,4,4,128]{5,4,3,2,1,0:T(4,128)}, f32[1,3,2,4,4,128...) custom-call(f32[1,3,2,4,4,128]{5,4,3,2,1,0:T(4,128)} %pos_in.1, ...), custom_call_target="tpu_custom_call" | custom-call | tf_op jit(solution)/shard_map/pallas_call | solution.py:422
  120.2 0.0 copy-start.1
  120.2 0.0 copy-done
  120.2 0.7 copy-done.1
  120.9 1.6 %multiply_add_fusion = (f32[1,3,2,4,4,128]{5,4,3,2,1,0:T(4,128)}, f32[1,3,2,4,4,128]{5,4,3,2,1,0:T(4,128)}, f32[1,3,2,4,4,128]{5,4,3,2,1,0:T(4,128)}, f32[1,3,2,4,4,128]{5,4,3,2,1,0:T(4,128)}) fusion(f32[1,3,2,4,4,128]{5,4,3,2,1,0:T(4,128)} %get-tuple-element.15, f32[1,1,3,2,4,4,128]{6,5,4,3,2,1,0:T(4,128)S(1)} %copy-done, ...), kind=kLoop, calls=%fused_computation.2 | loop fusion | flops 122880 | bytes 508416 | tf_op jit(solution)/shard_map/add | solution.py:465
  (1 shorter events, 0.0 us)
Async XLA Ops:
  2.1 118.2 %copy-start = (f32[1,1,3,2,4,4,128]{6,5,4,3,2,1,0:T(4,128)S(1)}, f32[1,1,3,2,4,4,128]{6,5,4,3,2,1,0:T(4,128)}, u32[]{:S(2)}) copy-start(f32[1,1,3,2,4,4,128]{6,5,4,3,2,1,0:T(4,128)} %param.8) | copy-start | bytes 147460
  120.2 0.7 copy-start.1
